TPU v7x, 32 devices: a whole 2x2x4 slice. The times are simulated.
32 devices in a mesh: dp: 16 (over z, y, core), tensor: 2 (over x).
Axes of the slice: x: 2, y: 2, z: 4, core: 2. Of those that a mesh axis runs over, the one named last changes fastest.
Arguments:
- tokens: bfloat16 [6144, 4096], P('dp'), may hold values from -6 to 6
- doc_lengths: int32 [32], P('dp'), may hold values from 1 to 192, as said below
- gate_weight: bfloat16 [4096, 7168], P('dp', 'tensor'), may hold values from -0.09375 to 0.09375
- up_weight: bfloat16 [4096, 7168], P('dp', 'tensor'), may hold values from -0.09375 to 0.09375
- hidden_grad: bfloat16 [6144, 7168], P('dp', 'tensor'), may hold values from -6 to 6
- in_projector: bfloat16 [64, 4096], replicated, may hold values from -0.09375 to 0.09375
- gate_projector: bfloat16 [64, 7168], P(None, 'tensor'), may hold values from -0.0625 to 0.0625
- up_projector: bfloat16 [64, 7168], P(None, 'tensor'), may hold values from -0.0625 to 0.0625
Outputs:
- gate_features: float32 [32, 64, 64], P('dp', None, 'tensor')
- up_features: float32 [32, 64, 64], P('dp', None, 'tensor')
Inputs may be any that keep to these rules, and one draw needn't show every extreme that they name: `doc_lengths`: at least one document in every draw has all 192 slots used.
All inputs are finite; a program needn't handle non-finite values.
Results may differ from a plain program's by a relative error of at most 0.013.
Values may be sent and summed in bfloat16 or wider, within the bound.
No kernel may reach another device: no remote copies, remote signals or barrier semaphores. Data moves between devices by JAX's collectives and lax.ppermute only.
A program may use at most 128 MiB of HBM per device.

v0:
```python
import jax
import jax.numpy as jnp
from jax import lax
from jax.sharding import PartitionSpec as P

DOC_LEN = 192


def contract_last(left, right):
    return lax.dot_general(
        left, right, (((1,), (1,)), ((), ())), preferred_element_type=jnp.float32
    )


def add_rows(whole, piece):
    return jnp.dot(whole, piece, preferred_element_type=jnp.float32)


def per_document(inputs, side):
    docs = inputs.shape[0] // DOC_LEN
    left = inputs.reshape(docs, DOC_LEN, inputs.shape[1])
    right = side.reshape(docs, DOC_LEN, side.shape[1])
    return 0.0625 * jnp.einsum("ntr,nts->nrs", left, right, preferred_element_type=jnp.float32)


def shards(
    tokens,
    doc_lengths,
    gate_weight,
    up_weight,
    hidden_grad,
    in_projector,
    gate_projector,
    up_projector,
):

    def add_one(piece):
        return add_rows(tokens, piece)

    gate = add_one(lax.all_gather(gate_weight, "dp", axis=0, tiled=True))
    up = add_one(lax.all_gather(up_weight, "dp", axis=0, tiled=True))
    sig = jax.nn.sigmoid(gate)
    cotangent = hidden_grad.astype(jnp.float32)
    grad_gate = (cotangent * up * sig * (1.0 + gate * (1.0 - sig))).astype(jnp.bfloat16)
    grad_up = (cotangent * gate * sig).astype(jnp.bfloat16)
    rows = tokens.shape[0]
    within = jnp.arange(rows, dtype=jnp.int32) % DOC_LEN
    limits = jnp.repeat(doc_lengths, DOC_LEN)
    mask = (within < limits).astype(jnp.bfloat16)
    projected = contract_last(tokens, in_projector)
    inputs = projected.astype(jnp.bfloat16) * mask[:, None]
    gate_part = contract_last(grad_gate, gate_projector)
    up_part = contract_last(grad_up, up_projector)
    gate_full, up_full = lax.psum((gate_part, up_part), "tensor")
    share = gate_full.shape[1] // lax.axis_size("tensor")
    start = lax.axis_index("tensor") * share
    gate_sum = lax.dynamic_slice_in_dim(gate_full, start, share, 1)
    up_sum = lax.dynamic_slice_in_dim(up_full, start, share, 1)
    gate_side = gate_sum.astype(jnp.bfloat16)
    up_side = up_sum.astype(jnp.bfloat16)
    return (per_document(inputs, gate_side), per_document(inputs, up_side))


def solution(mesh):
    placed = (
        P("dp", None),
        P("dp"),
        P("dp", "tensor"),
        P("dp", "tensor"),
        P("dp", "tensor"),
        P(),
        P(None, "tensor"),
        P(None, "tensor"),
    )
    return jax.shard_map(
        shards,
        mesh=mesh,
        in_specs=placed,
        out_specs=(P("dp", None, "tensor"), P("dp", None, "tensor")),
        check_vma=False,
    )
```

profile of v0, /device:TPU:0, one launch (start us, length us, event | category | flops | bytes accessed | tf_op | source)
XLA Modules:
  0.0 349.8 jit_solution(7200915189952742190)
XLA Ops:
  7.2 0.0 copy-start
  7.2 0.0 all-gather.5.cloned.1.call-start
  7.2 0.7 all-gather.5.cloned.1.call-update
  7.9 0.0 all-gather.3.cloned.1.call-start
  8.0 0.7 all-gather.3.cloned.1.call-update
  8.7 0.7 broadcast_in_dim.4
  9.4 0.1 reshape.32
  9.5 0.0 copy-done
  9.5 2.1 fusion.7
  11.6 0.1 reshape.33
  11.7 149.0 %all-gather.5.cloned.1.call-done = bf16[4096,3584]{1,0:T(8,128)(2,1)} async-done(((bf16[256,3584]{1,0:T(8,128)(2,1)}), bf16[4096,3584]{1,0:T(8,128)(2,1)}) %all-gather.5.cloned.1.call-update) | async-done | bytes 29360144 | tf_op jit(solution)/shard_map/all_gather | solution.py:40
  160.7 16.4 %fusion.18 = f32[384,3584]{1,0:T(8,128)S(1)} fusion(bf16[384,4096]{1,0:T(8,128)(2,1)S(1)} %copy-done, bf16[4096,3584]{1,0:T(8,128)(2,1)} %all-gather.5.cloned.1.call-done), kind=kOutput, calls=%fused_computation.27 | convolution fusion | flops 11274289152 | bytes 38010880 | tf_op jit(solution)/shard_map/dot_general | solution.py:16
  177.1 0.0 copy-start.3
  177.2 2.4 copy-done.3
  179.6 0.0 copy-done.1
  179.6 0.0 copy-done.2
  179.6 1.6 fusion.5
  181.2 129.4 %all-gather.3.cloned.1.call-done = bf16[4096,3584]{1,0:T(8,128)(2,1)} async-done(((bf16[256,3584]{1,0:T(8,128)(2,1)}), bf16[4096,3584]{1,0:T(8,128)(2,1)}) %all-gather.3.cloned.1.call-update) | async-done | bytes 29360144 | tf_op jit(solution)/shard_map/all_gather | solution.py:41
  310.7 19.8 %fusion.19 = f32[384,64]{0,1:T(8,128)S(1)} fusion(bf16[64,3584]{1,0:T(8,128)(2,1)} %param.14, bf16[384,4096]{1,0:T(8,128)(2,1)S(1)} %copy-done, bf16[4096,3584]{1,0:T(8,128)(2,1)} %all-gather.3.cloned.1.call-done, bf16[384,3584]{1,0:T(8,128)(2,1)} %param.12, f32[384,3584]{1,0:T(8,128)} %copy-done.3), kind=kOutput, calls=%fused_computation.28 | convolution fusion | flops 11465588736 | bytes 41320448 | tf_op jit(solution)/shard_map/dot_general | solution.py:10
  330.5 10.8 %all-reduce.2 = (bf16[384,64]{0,1:T(8,128)(2,1)S(1)}, bf16[384,64]{0,1:T(8,128)(2,1)S(1)}) all-reduce(f32[384,64]{0,1:T(8,128)S(1)} %fusion.19, f32[384,64]{0,1:T(8,128)S(1)} %fusion.5), channel_id=1, replica_groups=mesh['dp'=16,'tensor'=2] {'tensor'}, use_global_device_ids=true, to_apply=%region_0.1 | all-reduce | flops 49152 | bytes 294912 | tf_op jit(solution)/shard_map/psum | solution.py:54
  341.3 0.1 reshape.35
  341.4 0.1 reshape.34
  341.5 0.8 convolution_multiply_fusion
  342.2 0.8 convolution_multiply_fusion.1
  (4 shorter events, 0.0 us)
Async XLA Ops:
  7.2 2.3 copy-start
  7.2 153.5 %all-gather.5.cloned.1.call-start = ((), (), s32[]{:S(2)}) async-start(), calls=%async_computation.1 | async-start | bytes 31195136 | tf_op jit(solution)/shard_map/all_gather | solution.py:40
  7.9 302.7 %all-gather.3.cloned.1.call-start = ((), (), s32[]{:S(2)}) async-start(), calls=%async_computation | async-start | bytes 31195136 | tf_op jit(solution)/shard_map/all_gather | solution.py:41
  160.7 18.9 %copy-start.1 = (bf16[384,3584]{1,0:T(8,128)(2,1)S(1)}, bf16[384,3584]{1,0:T(8,128)(2,1)}, u32[]{:S(2)}) copy-start(bf16[384,3584]{1,0:T(8,128)(2,1)} %param.12) | copy-start | bytes 8257540
  160.7 18.9 %copy-start.2 = (bf16[64,3584]{1,0:T(8,128)(2,1)S(1)}, bf16[64,3584]{1,0:T(8,128)(2,1)}, u32[]{:S(2)}) copy-start(bf16[64,3584]{1,0:T(8,128)(2,1)} %param.15) | copy-start | bytes 1376260
  177.1 2.4 copy-start.3
Sparse Core Ops, SparseCore 0:
  9.6 151.0 all-gather.4
  162.3 148.3 all-gather.2
where the time goes:
time: 350 us
  waiting for transfers between devices  280 us (80%)
  matrix products  41.5 us (12%)
  between operations  14.1 us (4%)
  blocking collectives  10.8 us (3%)
  local copies, waits for them, and re-layouts  3.54 us (1%)
    all_gather x1, waiting for transfers between devices, shards(): gate = add_one(lax.all_gather(gate_weight, 'dp', axis=0, tiled=True))  149 us
    all_gather x1, waiting for transfers between devices, shards(): up = add_one(lax.all_gather(up_weight, 'dp', axis=0, tiled=True))  129 us
    dot_general x3, matrix products, contract_last(): lax.dot_general(left, right, (((1,), (1,)), ((), ())), preferred_element_...  23.6 us
    dot_general x1, matrix products, add_rows(): return jnp.dot(whole, piece, preferred_element_type=jnp.float32)  16.4 us
    psum x1, blocking collectives, shards(): gate_full, up_full = lax.psum((gate_part, up_part), 'tensor')  10.8 us
  transfers between devices with their start and end apart: 2, of which 2 were waited for; matrix products, arithmetic and copies ran while one was open for 6% of the time, Pallas kernels for 0%

commit v1 on v0

--- a/solution.py
+++ b/solution.py
@@ -1,19 +1,22 @@
+import functools
+
 import jax
 import jax.numpy as jnp
 from jax import lax
+from jax.experimental import pallas as pl
+from jax.experimental.pallas import tpu as pltpu
 from jax.sharding import PartitionSpec as P
 
 DOC_LEN = 192
+VMEM_LIMIT = 46 * 1024 * 1024
+UNITS = 7
+UNITS_A = 3
 
 
 def contract_last(left, right):
     return lax.dot_general(
         left, right, (((1,), (1,)), ((), ())), preferred_element_type=jnp.float32
     )
-
-
-def add_rows(whole, piece):
-    return jnp.dot(whole, piece, preferred_element_type=jnp.float32)
 
 
 def per_document(inputs, side):
@@ -23,7 +26,7 @@
     return 0.0625 * jnp.einsum("ntr,nts->nrs", left, right, preferred_element_type=jnp.float32)
 
 
-def shards(
+def shards_any(
     tokens,
     doc_lengths,
     gate_weight,
@@ -33,9 +36,8 @@
     gate_projector,
     up_projector,
 ):
-
     def add_one(piece):
-        return add_rows(tokens, piece)
+        return jnp.dot(tokens, piece, preferred_element_type=jnp.float32)
 
     gate = add_one(lax.all_gather(gate_weight, "dp", axis=0, tiled=True))
     up = add_one(lax.all_gather(up_weight, "dp", axis=0, tiled=True))
@@ -61,6 +63,500 @@
     return (per_document(inputs, gate_side), per_document(inputs, up_side))
 
 
+def vmem_spec():
+    return pl.BlockSpec(memory_space=pltpu.VMEM)
+
+
+def hbm_spec():
+    return pl.BlockSpec(memory_space=pltpu.HBM)
+
+
+def smem_spec():
+    return pl.BlockSpec(memory_space=pltpu.SMEM)
+
+
+def ffn_kernel(cfg, idx, *refs):
+    refs = list(refs)
+    groups, final = cfg["groups"], cfg["final"]
+    block_refs = [refs.pop(0) for _ in range(cfg["n_blocks"])]
+    token_refs = [refs.pop(0) for _ in range(cfg["n_tokens"])]
+    held = [refs.pop(0) for _ in cfg["held"]]
+    if final:
+        grad_refs = [refs.pop(0) for _ in cfg["grads"]]
+        gate_proj, up_proj = refs.pop(0), refs.pop(0)
+    prev = [refs.pop(0) for _ in range(cfg["prev"])]
+    outs = [refs.pop(0) for _ in range(cfg["n_outs"])]
+    block_buffer, block_sem = refs.pop(0), refs.pop(0)
+    token_buffer, token_sem = refs.pop(0), refs.pop(0)
+    if held:
+        held_buffer, held_sem = refs.pop(0), refs.pop(0)
+    if final:
+        grad_buffer, grad_sem = refs
+    else:
+        out_buffer, out_sem = refs
+    core = idx[0]
+    deep, width, rows = cfg["deep"], cfg["width"], cfg["rows"]
+
+    def token_copy(slot, unit, at):
+        g, d = unit
+        ref, z = token_refs[cfg["tokens"][g][d]], idx[1 + cfg["planes"][at]]
+        if len(ref.shape) == 2:
+            source = ref.at[:, pl.ds(pl.multiple_of(z * deep, deep), deep)]
+        else:
+            start = pl.multiple_of((z % 2) * deep, deep)
+            source = ref.at[2 * (core ^ (d & 1)) + z // 2, :, pl.ds(start, deep)]
+        return pltpu.make_async_copy(source, token_buffer.at[slot], token_sem.at[slot])
+
+    def arrived(buffer, sem, slot):
+        pltpu.make_async_copy(buffer.at[slot], buffer.at[slot], sem.at[slot]).wait()
+
+    def out_copy(n):
+        return pltpu.make_async_copy(out_buffer.at[n % 2], outs[0].at[n], out_sem.at[n % 2])
+
+    kept = [ref.at[i] for ref, count in zip(held, cfg["held"]) for i in range(count)]
+    kept = [kept[i] for i in cfg["order"]]
+
+    def grad_copy(n, unit):
+        ref, (row, column) = grad_refs[4 * unit[0] + unit[1]], cfg["grads"][4 * unit[0] + unit[1]]
+        source = ref.at[pl.ds(row, rows), pl.ds(column, width)]
+        return pltpu.make_async_copy(source, grad_buffer.at[n], grad_sem.at[n])
+
+    def finish(group, r, n, both):
+        s, d = group["units"][0]
+        d = d + r
+        arrived(grad_buffer, grad_sem, n)
+        gate, up = both[:, :width], both[:, width:]
+        sig = 1.0 / (1.0 + jnp.exp(-gate))
+        cotangent = grad_buffer[n].astype(jnp.float32)
+        grad_gate = (cotangent * up * sig * (1.0 + gate * (1.0 - sig))).astype(jnp.bfloat16)
+        grad_up = (cotangent * gate * sig).astype(jnp.bfloat16)
+        part = contract_last(gate_proj[...], grad_gate)
+        part += contract_last(up_proj[...], grad_up)
+        outs[s][d] = prev[s][d] + part if s < len(prev) else part
+
+    def work():
+        slot, n_kept, n, asked = 0, 0, 0, set()
+        for group in groups:
+            for unit in group["units"]:
+                for at in group["blocks"]:
+                    if at not in asked:
+                        asked.add(at)
+                        pltpu.make_async_copy(
+                            block_refs[at], block_buffer.at[at], block_sem.at[at]
+                        ).start()
+                    token_copy(slot, unit, at).start()
+                    slot += 1
+                if group["held"]:
+                    pltpu.make_async_copy(
+                        kept[n_kept], held_buffer.at[n_kept], held_sem.at[n_kept]
+                    ).start()
+                    n_kept += 1
+                if final:
+                    grad_copy(n, unit).start()
+                n += 1
+        slot, n_kept, first, here = 0, 0, 0, set()
+        for group in groups:
+            size, count = len(group["blocks"]), len(group["units"])
+            fresh = [at for at in group["blocks"] if at not in here]
+            here.update(fresh)
+
+            def unit_step(
+                r, carry, group=group, size=size, fresh=fresh, slot=slot, n_kept=n_kept, first=first
+            ):
+                both = None
+                for i, at in enumerate(group["blocks"]):
+                    if at in fresh:
+
+                        @pl.when(r == 0)
+                        def _(at=at):
+                            arrived(block_buffer, block_sem, at)
+
+                    arrived(token_buffer, token_sem, slot + r * size + i)
+                    term = jnp.dot(
+                        token_buffer[slot + r * size + i],
+                        block_buffer[at],
+                        preferred_element_type=jnp.float32,
+                    )
+                    both = term if both is None else both + term
+                if group["held"]:
+                    arrived(held_buffer, held_sem, n_kept + r)
+                    both = both + held_buffer[n_kept + r].astype(jnp.float32)
+                n = first + r
+                if final:
+                    finish(group, r, n, both)
+                else:
+
+                    @pl.when(n >= 2)
+                    def _():
+                        out_copy(n - 2).wait()
+
+                    out_buffer[n % 2] = both.astype(out_buffer.dtype)
+                    out_copy(n).start()
+                return carry
+
+            lax.fori_loop(0, count, unit_step, 0)
+            slot, first = slot + size * count, first + count
+            if group["held"]:
+                n_kept += count
+        if not final:
+            out_copy(first - 2).wait()
+            out_copy(first - 1).wait()
+
+    runs = idx[5] == cfg["inner"]
+    pl.when(runs)(work)
+
+    if final:
+
+        @pl.when(jnp.logical_not(runs))
+        def _():
+            for s, out in enumerate(outs):
+                out[...] = prev[s][...] if s < len(prev) else jnp.zeros_like(out)
+
+
+TOKENS = ((0, 1, 2, 2), (3, 3, 4, 4))
+
+
+def group(units, blocks, held=False):
+    return {"units": units, "blocks": blocks, "held": held}
+
+
+def ffn(idx, inner, blocks, tokens, groups, held, grads, proj, prev, name, order=None):
+    deep, width = blocks[0][0].shape[0], blocks[0][0].shape[1] // 2
+    rows = tokens[0].shape[-2]
+    final = grads is not None
+    n_units = sum(len(one["units"]) for one in groups)
+    cfg = {
+        "inner": inner,
+        "planes": [plane for _, plane in blocks],
+        "tokens": TOKENS,
+        "n_blocks": len(blocks),
+        "n_tokens": len(tokens),
+        "groups": groups,
+        "held": [value.shape[0] for value in held],
+        "order": order or range(sum(value.shape[0] for value in held)),
+        "grads": [place for _, *place in grads or ()],
+        "final": final,
+        "n_outs": len(grads) // 4 if final else 1,
+        "prev": len(prev),
+        "deep": deep,
+        "width": width,
+        "rows": rows,
+    }
+    large = [*(block for block, _ in blocks), *tokens, *held, *(one[0] for one in grads or ())]
+    args = [pltpu.with_memory_space_constraint(value, pltpu.HBM) for value in large]
+    specs = [hbm_spec()] * len(args)
+    args += [*(proj if final else ()), *prev]
+    specs += [vmem_spec()] * (len(args) - len(specs))
+    if final:
+        shapes = [(4, proj[0].shape[0], rows)] * (len(grads) // 4)
+    else:
+        shapes = [(n_units, rows, 2 * width)]
+    if final:
+        results = [jax.ShapeDtypeStruct(shape, jnp.float32) for shape in shapes]
+    else:
+        results = [pltpu.HBM(shape, jnp.bfloat16) for shape in shapes]
+
+    def buffers(count, shape, dtype, first=rows):
+        return [pltpu.VMEM((count, first, shape), dtype), pltpu.SemaphoreType.DMA((count,))]
+
+    slots = sum(len(one["units"]) * len(one["blocks"]) for one in groups)
+    scratch = buffers(len(blocks), 2 * width, jnp.bfloat16, deep)
+    scratch += buffers(slots, deep, jnp.bfloat16)
+    if held:
+        scratch += buffers(sum(cfg["held"]), 2 * width, jnp.bfloat16)
+    if final:
+        scratch += buffers(n_units, width, jnp.bfloat16)
+    else:
+        scratch += buffers(2, 2 * width, jnp.bfloat16)
+    parts = pl.pallas_call(
+        functools.partial(ffn_kernel, cfg),
+        out_shape=results,
+        in_specs=[smem_spec()] + specs,
+        out_specs=[vmem_spec() if final else hbm_spec()] * len(shapes),
+        scratch_shapes=scratch,
+        compiler_params=pltpu.CompilerParams(vmem_limit_bytes=VMEM_LIMIT),
+        cost_estimate=pl.CostEstimate(flops=1, bytes_accessed=1, transcendentals=0),
+        name=name,
+    )(idx, *args)
+    return list(parts)
+
+
+def features_kernel(docs, mine, sent, projected, limits, gate_out, up_out):
+    side = (mine[...] + sent[...].astype(jnp.float32)).astype(jnp.bfloat16)
+    share = side.shape[0] // 2
+    inputs = projected[...].astype(jnp.bfloat16)
+    position = lax.broadcasted_iota(jnp.int32, inputs.shape, 1)
+    for n in range(docs):
+        within = position - n * DOC_LEN
+        used = jnp.logical_and(within >= 0, within < limits[n])
+        left = jnp.where(used, inputs, jnp.zeros_like(inputs))
+        gate_out[n] = 0.0625 * contract_last(side[:share], left)
+        up_out[n] = 0.0625 * contract_last(side[share:], left)
+
+
+def shards_planes(
+    tokens,
+    doc_lengths,
+    gate_weight,
+    up_weight,
+    hidden_grad,
+    in_projector,
+    gate_projector,
+    up_projector,
+):
+    dp, x = lax.axis_index("dp"), lax.axis_index("tensor")
+    z, q = dp // 4, dp % 4
+    inner = jnp.logical_or(z == 1, z == 2).astype(jnp.int32)
+    first_pair = z < 2
+    far_inner = jnp.where(first_pair, 2, 1)
+    far_outer = jnp.where(first_pair, 3, 0)
+    y, core = (dp // 2) % 2, dp % 2
+    idx = jnp.stack([core, z, z ^ 1, far_inner, far_outer, inner]).astype(jnp.int32)
+
+    def planes(pairs):
+        return [(4 * a + i, 4 * b + i) for a, b in pairs for i in range(4)]
+
+    inward, outward = planes([(0, 1), (3, 2)]), planes([(1, 0), (2, 3)])
+    middle, neighbours = planes([(1, 2), (2, 1)]), planes([(0, 1), (1, 0), (2, 3), (3, 2)])
+
+    def move(value, perm):
+        return lax.ppermute(value, "dp", perm)
+
+    def flip(value, d):
+        return lax.ppermute(value, "dp", [(i, i ^ d) for i in range(16)])
+
+    def across(value):
+        return lax.ppermute(value, "tensor", [(0, 1), (1, 0)])
+
+    def gather_chips(value):
+        groups = [[4 * pair + i for i in range(4)] for pair in range(8)]
+        return lax.all_gather(value, ("dp", "tensor"), axis_index_groups=groups)
+
+    rows, model = tokens.shape
+    depth, hidden = gate_weight.shape
+    quarter = hidden // 4
+    cut = quarter // UNITS * UNITS_A
+    chunk_a, chunk_b = slice(0, cut), slice(cut, quarter)
+    ranks = gate_projector.shape[0]
+    share = ranks // 2
+
+    clock = idx
+
+    def wait(*values):
+        nonlocal clock
+        *values, clock = lax.optimization_barrier((*values, clock))
+        return values[0] if len(values) == 1 else values
+
+    def quarter_of(value, d):
+        return lax.dynamic_slice_in_dim(value, (q ^ d) * quarter, quarter, 1)
+
+    def weights_for(d, chunk):
+        gate, up = quarter_of(gate_weight, d), quarter_of(up_weight, d)
+        return jnp.concatenate([gate[:, chunk], up[:, chunk]], axis=1)
+
+    def grads_for(d, chunk):
+        return quarter_of(hidden_grad, d)[:, chunk]
+
+    def by_core(mine, other):
+        first, second = jnp.where(core == 0, mine, other), jnp.where(core == 0, other, mine)
+        return jnp.concatenate([first, second], axis=0)
+
+    def by_y(mine, other, columns):
+        mine, other = mine[:, columns], other[:, columns]
+        first, second = jnp.where(y == 0, mine, other), jnp.where(y == 0, other, mine)
+        return jnp.concatenate([first, second], axis=0)
+
+    gate_mine = lax.dynamic_slice_in_dim(gate_projector, q * quarter, quarter, 1)
+    up_mine = lax.dynamic_slice_in_dim(up_projector, q * quarter, quarter, 1)
+    nothing = jnp.zeros((share, quarter), jnp.bfloat16)
+    gate_rows = jnp.concatenate([gate_mine[:share], nothing, gate_mine[share:], nothing], axis=0)
+    up_rows = jnp.concatenate([nothing, up_mine[:share], nothing, up_mine[share:]], axis=0)
+    proj_a = [gate_rows[:, chunk_a], up_rows[:, chunk_a]]
+    proj_b = [gate_rows[:, chunk_b], up_rows[:, chunk_b]]
+
+    wide_a, wide_b = slice(0, 2 * cut), slice(2 * cut, 2 * quarter)
+    both = [
+        jnp.concatenate([weights_for(d, chunk_a), weights_for(d, chunk_b)], axis=1) for d in range(4)
+    ]
+    half = lax.dynamic_slice_in_dim(tokens, x * (model // 2), model // 2, 1)
+    core_in = flip(both[1], 1)
+    both[2], both[3], half, core_in = wait(both[2], both[3], half, core_in)
+    side_in, cross_in = flip(both[2], 2), flip(both[3], 3)
+    end_half = move(half, inward)
+    u0 = by_core(both[0], core_in)
+    far_u0 = move(u0, middle)
+    core_tokens = flip(tokens, 1)
+    grads = [quarter_of(hidden_grad, d) for d in range(4)]
+    grads_out_a = [piece[:, chunk_a] for piece in grads[2:]]
+    grads_out_b = jnp.stack([piece[:, chunk_b] for piece in grads[2:]])
+    core_grads = flip(grads[1], 1)
+    projected = contract_last(in_projector, tokens)
+
+    side_in, cross_in, far_u0, end_half, half, core_tokens, projected = wait(
+        side_in, cross_in, far_u0, end_half, half, core_tokens, projected
+    )
+    grads_out_a[0], grads_out_a[1], grads_out_b, core_grads, grads[0] = wait(
+        *grads_out_a, grads_out_b, core_grads, grads[0]
+    )
+    proj_a[0], proj_a[1], proj_b[0], proj_b[1] = wait(*proj_a, *proj_b)
+    u1 = by_core(side_in, cross_in)
+    far_u1 = move(u1, middle)
+    whole_a = by_y(u0, u1, wide_a)
+    end_a = move(whole_a, neighbours)
+    side_half = flip(half, 2)
+    end_all = gather_chips(end_half)
+    whole_b = by_y(u0, u1, wide_b)
+
+    far_u1, end_a, side_half, whole_b, end_half, grads_out_b = wait(
+        far_u1, end_a, side_half, whole_b, end_half, grads_out_b
+    )
+    far_end_a = move(end_a, middle)
+    end_b = move(whole_b, inward)
+    side_end_half = flip(end_half, 2)
+    side_grads_b = flip(grads_out_b, 2)
+    far_a, far_b = by_y(far_u0, far_u1, wide_a), by_y(far_u0, far_u1, wide_b)
+    out_a = move(far_a, outward)
+    side_all = gather_chips(side_half)
+
+    own, end = [(0, d) for d in range(4)], [(1, d) for d in range(4)]
+    rows_in = [tokens, core_tokens, tokens, end_all]
+
+    (held_b,) = ffn(
+        clock,
+        1,
+        [(whole_b, 0), (far_b, 2)],
+        rows_in,
+        [group(own[:2] + end[:2], (0, 1))],
+        [],
+        None,
+        None,
+        [],
+        "b_first",
+    )
+    (held_a,) = ffn(
+        clock,
+        1,
+        [(whole_a, 0), (end_a, 1), (far_a, 2)],
+        [tokens, core_tokens],
+        [group(own[:2], (0, 1, 2))],
+        [],
+        None,
+        None,
+        [],
+        "a_first",
+    )
+    held_a, held_b, side_all, end_all, side_end_half, side_grads_b, *moved = wait(
+        held_a,
+        held_b,
+        side_all,
+        end_all,
+        side_end_half,
+        side_grads_b,
+        grads_out_a[0],
+        grads_out_a[1],
+        far_end_a,
+        end_b,
+        out_a,
+    )
+    *grads_out_a, far_end_a, end_b, out_a = moved
+    far_end_b = move(end_b, middle)
+    out_end_a = move(far_end_a, outward)
+    side_grads_a = [flip(grads_out_a[0], 2), flip(grads_out_a[1], 3)]
+    side_end_all = gather_chips(side_end_half)
+    pieces = [grads[0][:, chunk_b], core_grads[:, chunk_b], side_grads_b[0]]
+    own_grads_b = jnp.concatenate([*pieces, flip(side_grads_b[1], 1)], axis=0)
+    end_grads_b = move(own_grads_b, inward)
+    rows_in = [tokens, core_tokens, side_all, end_all, end_all]
+    blocks_b = [(whole_b, 0), (end_b, 1), (far_b, 2)]
+    (held_b,) = ffn(
+        clock,
+        1,
+        blocks_b,
+        rows_in,
+        [group(own[:2] + end[:2], (1,), True), group(own[2:], (0, 1, 2))],
+        [held_b],
+        None,
+        None,
+        [],
+        "b_next",
+    )
+    blocks_a = [(whole_a, 0), (end_a, 1), (far_a, 2)]
+    (held_late,) = ffn(
+        clock, 1, blocks_a, rows_in[:3], [group(own[2:], (0, 1, 2))], [], None, None, [], "a_second"
+    )
+    held_b, held_late, *side_grads_a = wait(held_b, held_late, *side_grads_a)
+    grads_a = [(grads[0], 0, 0), (core_grads, 0, 0)] + [(piece, 0, 0) for piece in side_grads_a]
+    sums = ffn(
+        clock,
+        1,
+        [(far_end_a, 3)],
+        rows_in[:3],
+        [group(own, (0,), True)],
+        [held_a, held_late],
+        grads_a,
+        proj_a,
+        [],
+        "a_inner",
+    )
+    sums[0], side_end_all, out_end_a = wait(sums[0], side_end_all, out_end_a)
+    rows_in[4] = side_end_all
+
+    def ends_a(*values):
+        so_far, index, grads_a, rows_a, blocks = values[0], values[1], values[2:6], values[6:9], values[9:]
+        blocks = [(value, plane) for plane, value in enumerate(blocks)]
+        grads_a = [(piece, 0, 0) for piece in grads_a]
+        units = [group(own, (0, 1, 2, 3))]
+        return ffn(index, 0, blocks, rows_a, units, [], grads_a, proj_a, [so_far], "a_end")[0]
+
+    values = [sums[0], clock, *(piece for piece, _, _ in grads_a), *rows_in[:3]]
+    values += [whole_a, end_a, out_a, out_end_a]
+    sums = [lax.cond(inner == 1, lambda *values: values[0], ends_a, *values)]
+    sums[0], end_grads_b, far_end_b = wait(sums[0], end_grads_b, far_end_b)
+    grads_b = [(value, d * rows, 0) for value in (own_grads_b, end_grads_b) for d in range(4)]
+    sums = ffn(
+        clock,
+        1,
+        [*blocks_b, (far_end_b, 3)],
+        rows_in,
+        [group(own, (3,), True), group(end[:2], (3,), True), group(end[2:], (0, 1, 2, 3))],
+        [held_b],
+        grads_b,
+        proj_b,
+        sums,
+        "b_last",
+        order=(0, 1, 4, 5, 2, 3),
+    )
+
+    kept = jnp.stack([part[d] for part in sums for d in (0, 2)])
+    sent = jnp.stack([part[d] for part in sums for d in (1, 3)])
+    kept = kept + flip(sent, 1)
+    keep = lax.dynamic_slice_in_dim(kept, x * ranks, ranks, 1)
+    give = lax.dynamic_slice_in_dim(kept, (1 - x) * ranks, ranks, 1)
+    send = give.astype(jnp.bfloat16)
+    both_ways = [
+        (2 * i + t, 2 * (i ^ 2) + 1 - t) for i in range(16) for t in range(2)
+    ]
+    arrived = [
+        across(send[0::2]),
+        flip(keep[1::2].astype(jnp.bfloat16), 2),
+        lax.ppermute(send[1::2], ("dp", "tensor"), both_ways),
+    ]
+    total = keep[0::2]
+    for value in arrived:
+        total = total + value.astype(jnp.float32)
+    back = move(total[1].astype(jnp.bfloat16), outward)
+
+    docs = doc_lengths.shape[0]
+    gate_out, up_out = pl.pallas_call(
+        functools.partial(features_kernel, docs),
+        out_shape=[jax.ShapeDtypeStruct((docs, share, ranks), jnp.float32)] * 2,
+        in_specs=[vmem_spec()] * 3 + [smem_spec()],
+        out_specs=[vmem_spec()] * 2,
+        name="features",
+    )(total[0], back, projected, doc_lengths)
+    return jnp.swapaxes(gate_out, 1, 2), jnp.swapaxes(up_out, 1, 2)
+
+
 def solution(mesh):
     placed = (
         P("dp", None),
@@ -72,8 +568,9 @@
         P(None, "tensor"),
         P(None, "tensor"),
     )
+    planes = mesh.shape["dp"] == 16 and mesh.shape["tensor"] == 2
     return jax.shard_map(
-        shards,
+        shards_planes if planes else shards_any,
         mesh=mesh,
         in_specs=placed,
         out_specs=(P("dp", None, "tensor"), P("dp", None, "tensor")),

time: 350 us -> 274 us (0.78)
  waiting for transfers between devices: 280 us -> 147 us
  starting transfers between devices: 0.08 us -> 43.4 us
  matrix products: 41.5 us -> 3.61 us
  Pallas kernels: 0 us -> 28.1 us
  other arithmetic: 0.01 us -> 17 us
  local copies, waits for them, and re-layouts: 3.54 us -> 20 us
  blocking collectives: 10.8 us -> 0 us
    all_gather x2 -> x3, waiting for transfers between devices: 278 us -> 2.16 us  [gather_chips(): return lax.all_gather(value, ('dp', 'tensor'), axis_index_groups=groups)]
    ppermute x0 -> x26, waiting for transfers between devices: none -> 145 us  [the longest x13 90.6 us: flip(): return lax.ppermute(value, 'dp', [(i, i ^ d) for i in range(16)])]
    ppermute x0 -> x26, starting transfers between devices: none -> 43.3 us  [the longest x11 31.8 us: move(): return lax.ppermute(value, 'dp', perm)]
    pallas_call x0 -> x8, Pallas kernels: none -> 28.1 us  [the longest x7 26.4 us: ffn(): pl.pallas_call(functools.partial(ffn_kernel, cfg), out_shape=results, in_...]
    dot_general x3 -> x1, matrix products: 23.6 us -> 3.61 us  [contract_last(): lax.dot_general(left, right, (((1,), (1,)), ((), ())), preferred_element_...]
    dot_general x3 -> x0, matrix products: 18 us -> none  [the longest x1 16.4 us: add_rows(): return jnp.dot(whole, piece, preferred_element_type=jnp.float32)]
    psum x1 -> x0, blocking collectives: 10.8 us -> none  [shards(): gate_full, up_full = lax.psum((gate_part, up_part), 'tensor')]
    slice x0 -> x10, local copies, waits for them, and re-layouts: none -> 8.92 us  [the longest x2 4.85 us: weights_for(): return jnp.concatenate([gate[:, chunk], up[:, chunk]], axis=1)]
  transfers between devices with their start and end apart: 2 -> 29, of which waited for: 2 -> 13; matrix products, arithmetic and copies ran while one was open for 6% -> 12% of each run, Pallas kernels for 0% -> 9%
where the time goes in v1:
time: 274 us; the launch traced here: 273 us
  waiting for transfers between devices  147 us (54%)
  starting transfers between devices  43.4 us (16%)
  Pallas kernels  28.1 us (10%)
  local copies, waits for them, and re-layouts  20 us (7%)
  other arithmetic  17 us (6%)
  between operations  14.3 us (5%)
  matrix products  3.61 us (1%)
    ppermute x13, waiting for transfers between devices, flip(): return lax.ppermute(value, 'dp', [(i, i ^ d) for i in range(16)])  90.6 us
    ppermute x11, waiting for transfers between devices, move(): return lax.ppermute(value, 'dp', perm)  51.3 us
    ppermute x11, starting transfers between devices, move(): return lax.ppermute(value, 'dp', perm)  31.8 us
    pallas_call x7, Pallas kernels, ffn(): pl.pallas_call(functools.partial(ffn_kernel, cfg), out_shape=results, in_...  26.4 us
    ppermute x13, starting transfers between devices, flip(): return lax.ppermute(value, 'dp', [(i, i ^ d) for i in range(16)])  8.21 us
  transfers between devices with their start and end apart: 29, of which 13 were waited for; matrix products, arithmetic and copies ran while one was open for 12% of the time, Pallas kernels for 9%

profile of v1, /device:TPU:0, one launch (start us, length us, event | category | flops | bytes accessed | tf_op | source)
XLA Modules:
  0.0 273.5 jit_solution(2759470759777227686)
XLA Ops:
  7.3 2.7 constant_dynamic-slice_fusion.3
  10.0 2.2 constant_dynamic-slice_fusion.15
  14.2 2.8 %constant_dynamic-slice_fusion.19 = bf16[384,2048]{1,0:T(8,128)(2,1)} fusion(bf16[384,4096]{1,0:T(8,128)(2,1)} %refs_4_.3, s32[]{:T(128)S(6)} %select_n.134), kind=kLoop, calls=%fused_computation.74 | loop fusion | bytes 3145732 | tf_op jit(solution)/shard_map/dynamic_slice | solution.py:381
  20.8 1.9 collective-permute-start.3
  22.7 7.6 %collective-permute-start.4 = (bf16[384,2048]{1,0:T(8,128)(2,1)}, bf16[384,2048]{1,0:T(8,128)(2,1)}, u32[]{:S(2)}, u32[]{:S(2)}) collective-permute-start(bf16[384,2048]{1,0:T(8,128)(2,1)} %constant_dynamic-slice_fusion.19), channel_id=1, source_target_pairs={{0,8},{2,10},{4,12},{6,14},{24,16},{26,18},{28,20},{30,22},{1,9},{... | collective-permute-start | bytes 4718600 | tf_op jit(solution)/shard_map/ppermute | solution.py:323
  31.9 3.6 %fusion.9.projected = f32[64,384]{1,0:T(8,128)} fusion(bf16[64,4096]{1,0:T(8,128)(2,1)S(1)} %copy-done, bf16[384,4096]{1,0:T(8,128)(2,1)} %refs_4_.3), kind=kOutput, calls=%fused_computation.83 | convolution fusion | flops 201326592 | bytes 3768320 | tf_op jit(solution)/shard_map/dot_general | solution.py:17
  35.5 18.1 %collective-permute-done.1 = bf16[256,1792]{1,0:T(8,128)(2,1)S(1)} collective-permute-done((bf16[256,1792]{1,0:T(8,128)(2,1)S(1)}, bf16[256,1792]{1,0:T(8,128)(2,1)S(1)}, u32[]{:S(2)}, u32[]{:S(2)}) %collective-permute-start.1) | collective-permute-done | bytes 917536 | tf_op jit(solution)/shard_map/ppermute | solution.py:326
  53.6 17.2 %collective-permute-done.2 = bf16[256,1792]{1,0:T(8,128)(2,1)S(1)} collective-permute-done((bf16[256,1792]{1,0:T(8,128)(2,1)S(1)}, bf16[256,1792]{1,0:T(8,128)(2,1)S(1)}, u32[]{:S(2)}, u32[]{:S(2)}) %collective-permute-start.2) | collective-permute-done | bytes 917536 | tf_op jit(solution)/shard_map/ppermute | solution.py:326
  75.0 1.9 collective-permute-start.6
  82.9 1.9 constant_dynamic-slice_fusion.1
  87.9 28.0 %collective-permute-done.7.refs_1_ = bf16[1024,768]{1,0:T(8,128)(2,1)} collective-permute-done((bf16[1024,768]{1,0:T(8,128)(2,1)}, bf16[1024,768]{1,0:T(8,128)(2,1)}, u32[]{:S(2)}, u32[]{:S(2)}) %collective-permute-start.7) | collective-permute-done | bytes 1572896 | tf_op jit(solution)/shard_map/ppermute | solution.py:323
  116.0 5.8 %collective-permute-start.13 = (bf16[1024,1024]{1,0:T(8,128)(2,1)S(1)}, bf16[1024,1024]{1,0:T(8,128)(2,1)}, u32[]{:S(2)}, u32[]{:S(2)}) collective-permute-start(bf16[1024,1024]{1,0:T(8,128)(2,1)S(1)} %pad_maximum_fusion.2.refs_0_), channel_id=1, source_target_pairs={{0,8},{2,10},{4,12},{6,14},{24,16},{26,18},{28,20},{30,22},{1,9},{... | collective-permute-start | bytes 6291464 | tf_op jit(solution)/shard_map/ppermute | solution.py:323
  134.3 40.6 %collective-permute-done.11 = bf16[2,384,512]{2,1,0:T(8,128)(2,1)} collective-permute-done((bf16[2,384,512]{2,1,0:T(8,128)(2,1)S(1)}, bf16[2,384,512]{2,1,0:T(8,128)(2,1)}, u32[]{:S(2)}, u32[]{:S(2)}) %collective-permute-start.11) | collective-permute-done | bytes 786464 | tf_op jit(solution)/shard_map/ppermute | solution.py:326
  176.3 2.0 collective-permute-start.20
  180.9 6.8 %collective-permute-start.19 = (bf16[1536,512]{1,0:T(8,128)(2,1)S(1)}, bf16[1536,512]{1,0:T(8,128)(2,1)}, u32[]{:S(2)}, u32[]{:S(2)}) collective-permute-start(bf16[1536,512]{1,0:T(8,128)(2,1)S(1)} %pad_maximum_fusion.6.refs_10_.refs_11_.refs_12_.refs_13_), channel_id=1, source_target_pairs={{0,8},{2,10},{4,12},{6,14},{24,16},{26,18},{28,20},{30,22},{1,9},{... | collective-permute-start | bytes 4718600 | tf_op jit(solution)/shard_map/ppermute | solution.py:323
  190.9 6.7 %collective-permute-done.15.refs_8_ = bf16[384,384]{1,0:T(8,128)(2,1)S(1)} collective-permute-done((bf16[384,384]{1,0:T(8,128)(2,1)S(1)}, bf16[384,384]{1,0:T(8,128)(2,1)S(1)}, u32[]{:S(2)}, u32[]{:S(2)}) %collective-permute-start.15) | collective-permute-done | bytes 294944 | tf_op jit(solution)/shard_map/ppermute | solution.py:326
  197.6 4.4 %collective-permute-done.16.refs_9_ = bf16[384,384]{1,0:T(8,128)(2,1)S(1)} collective-permute-done((bf16[384,384]{1,0:T(8,128)(2,1)S(1)}, bf16[384,384]{1,0:T(8,128)(2,1)S(1)}, u32[]{:S(2)}, u32[]{:S(2)}) %collective-permute-start.16) | collective-permute-done | bytes 294944 | tf_op jit(solution)/shard_map/ppermute | solution.py:326
  203.5 15.0 %collective-permute-done.17 = bf16[1024,768]{1,0:T(8,128)(2,1)} collective-permute-done((bf16[1024,768]{1,0:T(8,128)(2,1)}, bf16[1024,768]{1,0:T(8,128)(2,1)}, u32[]{:S(2)}, u32[]{:S(2)}) %collective-permute-start.17) | collective-permute-done | bytes 1572896 | tf_op jit(solution)/shard_map/ppermute | solution.py:323
  218.5 2.1 all-gather.11.cloned.1.call-done
  220.6 21.7 %conditional.1 = (f32[4,128,384]{2,1,0:T(8,128)S(1)}) conditional(s32[]{:T(128)} %convert_element_type.24, (s32[6]{0:T(128)S(1)}, bf16[1024,768]{1,0:T(8,128)(2,1)}, bf16[1024,768]{1,0:T(8,128)(2,1)}, bf16[1024,768]{1,0:T(8,128)(2,1)}, bf16[1024,768]{1,0:T(8,128)(2,1)}, /*index=5*/bf16[384,4096]{1,0:T(8,128)(2,1)}, bf16[384,4096]{1,0:T(8,128)(2,1)}, ...), branch_computations={%region_0.1_spmd, %region_1.2_spmd} | conditional | flops 1 | bytes 1572873 | solution.py:513
  220.6 21.6 %a_end.1 = f32[4,128,384]{2,1,0:T(8,128)S(1)} custom-call(s32[6]{0:T(128)S(1)} %get-tuple-element.34.idx, bf16[1024,768]{1,0:T(8,128)(2,1)} %get-tuple-element.35.refs_0_, bf16[1024,768]{1,0:T(8,128)(2,1)} %get-tuple-element.36.refs_1_, bf16[1024,768]{1,0:T(8,128)(2,1)} %get-tuple-element.37.refs_2_, bf16[1024,768]{1,0:T(8,128)(2,1)} %get-tuple-element.38.refs_3_, ...), custom_call_target="tpu_custom_call" | custom-call | flops 1 | bytes 1 | tf_op jit(solution)/shard_map/cond/branch_0_fun/a_end/pallas_call | solution.py:271
  244.0 2.0 collective-permute-done.21
  249.9 2.7 %collective-permute-done.24 = bf16[2,64,384]{2,1,0:T(8,128)(2,1)S(1)} collective-permute-done((bf16[2,64,384]{2,1,0:T(8,128)(2,1)S(1)}, bf16[2,64,384]{2,1,0:T(8,128)(2,1)S(1)}, u32[]{:S(2)}, u32[]{:S(2)}) %collective-permute-start.24) | collective-permute-done | bytes 98336 | tf_op jit(solution)/shard_map/ppermute | solution.py:542
  256.3 8.3 %collective-permute-done.25.sent = bf16[64,384]{1,0:T(8,128)(2,1)S(1)} collective-permute-done((bf16[64,384]{1,0:T(8,128)(2,1)S(1)}, bf16[64,384]{1,0:T(8,128)(2,1)S(1)}, u32[]{:S(2)}, u32[]{:S(2)}) %collective-permute-start.25) | collective-permute-done | bytes 49184 | tf_op jit(solution)/shard_map/ppermute | solution.py:323
  (138 shorter events, 53.1 us)
Async XLA Ops:
  7.2 126.5 %all-gather.7.cloned.1.call-start = ((), (), s32[]{:S(2)}) async-start(), calls=%async_computation | async-start | bytes 7864320 | tf_op jit(solution)/shard_map/all_gather | solution.py:333
  12.7 59.1 %collective-permute-start.5 = (bf16[384,4096]{1,0:T(8,128)(2,1)}, bf16[384,4096]{1,0:T(8,128)(2,1)}, u32[]{:S(2)}, u32[]{:S(2)}) collective-permute-start(bf16[384,4096]{1,0:T(8,128)(2,1)} %refs_4_.3), channel_id=1, source_target_pairs={{0,2},{2,0},{4,6},{6,4},{8,10},{10,8},{12,14},{14,12},{16,18},{18,... | collective-permute-start | bytes 9437192 | tf_op jit(solution)/shard_map/ppermute | solution.py:326
  20.8 51.0 %collective-permute-start.3 = (bf16[512,1792]{1,0:T(8,128)(2,1)}, bf16[512,1792]{1,0:T(8,128)(2,1)}, u32[]{:S(2)}, u32[]{:S(2)}) collective-permute-start(bf16[512,1792]{1,0:T(8,128)(2,1)} %pad_maximum_fusion), channel_id=1, source_target_pairs={{8,16},{10,18},{12,20},{14,22},{16,8},{18,10},{20,12},{22,14},{9,1... | collective-permute-start | bytes 5505032 | tf_op jit(solution)/shard_map/ppermute | solution.py:323
  22.7 49.0 %collective-permute-start.4 = (bf16[384,2048]{1,0:T(8,128)(2,1)}, bf16[384,2048]{1,0:T(8,128)(2,1)}, u32[]{:S(2)}, u32[]{:S(2)}) collective-permute-start(bf16[384,2048]{1,0:T(8,128)(2,1)} %constant_dynamic-slice_fusion.19), channel_id=1, source_target_pairs={{0,8},{2,10},{4,12},{6,14},{24,16},{26,18},{28,20},{30,22},{1,9},{... | collective-permute-start | bytes 4718600 | tf_op jit(solution)/shard_map/ppermute | solution.py:323
  30.4 23.3 %collective-permute-start.1 = (bf16[256,1792]{1,0:T(8,128)(2,1)S(1)}, bf16[256,1792]{1,0:T(8,128)(2,1)S(1)}, u32[]{:S(2)}, u32[]{:S(2)}) collective-permute-start(bf16[256,1792]{1,0:T(8,128)(2,1)S(1)} %pad_maximum_fusion.7), channel_id=1, source_target_pairs={{0,4},{2,6},{4,0},{6,2},{8,12},{10,14},{12,8},{14,10},{16,20},{18,... | collective-permute-start | bytes 2752520 | tf_op jit(solution)/shard_map/ppermute | solution.py:326
  31.9 39.0 %collective-permute-start.2 = (bf16[256,1792]{1,0:T(8,128)(2,1)S(1)}, bf16[256,1792]{1,0:T(8,128)(2,1)S(1)}, u32[]{:S(2)}, u32[]{:S(2)}) collective-permute-start(bf16[256,1792]{1,0:T(8,128)(2,1)S(1)} %pad_maximum_fusion.8), channel_id=1, source_target_pairs={{0,6},{2,4},{4,2},{6,0},{8,14},{10,12},{12,10},{14,8},{16,22},{18,... | collective-permute-start | bytes 2752520 | tf_op jit(solution)/shard_map/ppermute | solution.py:326
  71.8 103.1 %all-gather.9.cloned.1.call-start = ((), (), s32[]{:S(2)}) async-start(), calls=%async_computation.1 | async-start | bytes 7864320 | tf_op jit(solution)/shard_map/all_gather | solution.py:333
  75.0 40.9 %collective-permute-start.6 = (bf16[512,1792]{1,0:T(8,128)(2,1)}, bf16[512,1792]{1,0:T(8,128)(2,1)}, u32[]{:S(2)}, u32[]{:S(2)}) collective-permute-start(bf16[512,1792]{1,0:T(8,128)(2,1)} %pad_maximum_fusion.1), channel_id=1, source_target_pairs={{8,16},{10,18},{12,20},{14,22},{16,8},{18,10},{20,12},{22,14},{9,1... | collective-permute-start | bytes 5505032 | tf_op jit(solution)/shard_map/ppermute | solution.py:323
  78.5 37.4 %collective-permute-start.7 = (bf16[1024,768]{1,0:T(8,128)(2,1)}, bf16[1024,768]{1,0:T(8,128)(2,1)}, u32[]{:S(2)}, u32[]{:S(2)}) collective-permute-start(bf16[1024,768]{1,0:T(8,128)(2,1)} %pad_maximum_fusion.4.refs_0_), channel_id=1, source_target_pairs={{0,8},{2,10},{4,12},{6,14},{8,0},{10,2},{12,4},{14,6},{16,24},{18,... | collective-permute-start | bytes 4718600 | tf_op jit(solution)/shard_map/ppermute | solution.py:323
  78.5 37.4 %collective-permute-start.8 = (bf16[384,2048]{1,0:T(8,128)(2,1)}, bf16[384,2048]{1,0:T(8,128)(2,1)}, u32[]{:S(2)}, u32[]{:S(2)}) collective-permute-start(bf16[384,2048]{1,0:T(8,128)(2,1)} %constant_dynamic-slice_fusion.19), channel_id=1, source_target_pairs={{0,4},{2,6},{4,0},{6,2},{8,12},{10,14},{12,8},{14,10},{16,20},{18,... | collective-permute-start | bytes 4718600 | tf_op jit(solution)/shard_map/ppermute | solution.py:326
  115.9 104.7 %all-gather.11.cloned.1.call-start = ((), (), s32[]{:S(2)}) async-start(), calls=%async_computation.2 | async-start | bytes 7864320 | tf_op jit(solution)/shard_map/all_gather | solution.py:333
  116.0 58.9 %collective-permute-start.13 = (bf16[1024,1024]{1,0:T(8,128)(2,1)S(1)}, bf16[1024,1024]{1,0:T(8,128)(2,1)}, u32[]{:S(2)}, u32[]{:S(2)}) collective-permute-start(bf16[1024,1024]{1,0:T(8,128)(2,1)S(1)} %pad_maximum_fusion.2.refs_0_), channel_id=1, source_target_pairs={{0,8},{2,10},{4,12},{6,14},{24,16},{26,18},{28,20},{30,22},{1,9},{... | collective-permute-start | bytes 6291464 | tf_op jit(solution)/shard_map/ppermute | solution.py:323
  121.8 53.1 %collective-permute-start.10 = (bf16[384,2048]{1,0:T(8,128)(2,1)}, bf16[384,2048]{1,0:T(8,128)(2,1)}, u32[]{:S(2)}, u32[]{:S(2)}) collective-permute-start(bf16[384,2048]{1,0:T(8,128)(2,1)} %collective-permute-done.4), channel_id=1, source_target_pairs={{0,4},{2,6},{4,0},{6,2},{8,12},{10,14},{12,8},{14,10},{16,20},{18,... | collective-permute-start | bytes 4718600 | tf_op jit(solution)/shard_map/ppermute | solution.py:326
  123.2 51.7 %collective-permute-start.12 = (bf16[1024,768]{1,0:T(8,128)(2,1)}, bf16[1024,768]{1,0:T(8,128)(2,1)}, u32[]{:S(2)}, u32[]{:S(2)}) collective-permute-start(bf16[1024,768]{1,0:T(8,128)(2,1)} %collective-permute-done.7.refs_1_), channel_id=1, source_target_pairs={{8,16},{10,18},{12,20},{14,22},{16,8},{18,10},{20,12},{22,14},{9,1... | collective-permute-start | bytes 4718600 | tf_op jit(solution)/shard_map/ppermute | solution.py:323
  127.9 46.9 %collective-permute-start.14 = (bf16[1024,768]{1,0:T(8,128)(2,1)}, bf16[1024,768]{1,0:T(8,128)(2,1)}, u32[]{:S(2)}, u32[]{:S(2)}) collective-permute-start(bf16[1024,768]{1,0:T(8,128)(2,1)} %pad_maximum_fusion.5.refs_2_), channel_id=1, source_target_pairs={{8,0},{10,2},{12,4},{14,6},{16,24},{18,26},{20,28},{22,30},{9,1},{... | collective-permute-start | bytes 4718600 | tf_op jit(solution)/shard_map/ppermute | solution.py:323
  129.2 45.6 %collective-permute-start.11 = (bf16[2,384,512]{2,1,0:T(8,128)(2,1)S(1)}, bf16[2,384,512]{2,1,0:T(8,128)(2,1)}, u32[]{:S(2)}, u32[]{:S(2)}) collective-permute-start(bf16[2,384,512]{2,1,0:T(8,128)(2,1)S(1)} %copy-done.16), channel_id=1, source_target_pairs={{0,4},{2,6},{4,0},{6,2},{8,12},{10,14},{12,8},{14,10},{16,20},{18,... | collective-permute-start | bytes 2359304 | tf_op jit(solution)/shard_map/ppermute | solution.py:326
  176.3 66.0 %collective-permute-start.20 = (bf16[1024,1024]{1,0:T(8,128)(2,1)}, bf16[1024,1024]{1,0:T(8,128)(2,1)}, u32[]{:S(2)}, u32[]{:S(2)}) collective-permute-start(bf16[1024,1024]{1,0:T(8,128)(2,1)} %collective-permute-done.13.refs_1_), channel_id=1, source_target_pairs={{8,16},{10,18},{12,20},{14,22},{16,8},{18,10},{20,12},{22,14},{9,1... | collective-permute-start | bytes 6291464 | tf_op jit(solution)/shard_map/ppermute | solution.py:323
  179.3 39.1 %collective-permute-start.17 = (bf16[1024,768]{1,0:T(8,128)(2,1)}, bf16[1024,768]{1,0:T(8,128)(2,1)}, u32[]{:S(2)}, u32[]{:S(2)}) collective-permute-start(bf16[1024,768]{1,0:T(8,128)(2,1)} %collective-permute-done.12.refs_0_), channel_id=1, source_target_pairs={{8,0},{10,2},{12,4},{14,6},{16,24},{18,26},{20,28},{22,30},{9,1},{... | collective-permute-start | bytes 4718600 | tf_op jit(solution)/shard_map/ppermute | solution.py:323
  180.9 61.4 %collective-permute-start.19 = (bf16[1536,512]{1,0:T(8,128)(2,1)S(1)}, bf16[1536,512]{1,0:T(8,128)(2,1)}, u32[]{:S(2)}, u32[]{:S(2)}) collective-permute-start(bf16[1536,512]{1,0:T(8,128)(2,1)S(1)} %pad_maximum_fusion.6.refs_10_.refs_11_.refs_12_.refs_13_), channel_id=1, source_target_pairs={{0,8},{2,10},{4,12},{6,14},{24,16},{26,18},{28,20},{30,22},{1,9},{... | collective-permute-start | bytes 4718600 | tf_op jit(solution)/shard_map/ppermute | solution.py:323
  187.7 9.9 %collective-permute-start.15 = (bf16[384,384]{1,0:T(8,128)(2,1)S(1)}, bf16[384,384]{1,0:T(8,128)(2,1)S(1)}, u32[]{:S(2)}, u32[]{:S(2)}) collective-permute-start(bf16[384,384]{1,0:T(8,128)(2,1)S(1)} %copy-done.22), channel_id=1, source_target_pairs={{0,4},{2,6},{4,0},{6,2},{8,12},{10,14},{12,8},{14,10},{16,20},{18,... | collective-permute-start | bytes 884744 | tf_op jit(solution)/shard_map/ppermute | solution.py:326
  189.3 12.7 %collective-permute-start.16 = (bf16[384,384]{1,0:T(8,128)(2,1)S(1)}, bf16[384,384]{1,0:T(8,128)(2,1)S(1)}, u32[]{:S(2)}, u32[]{:S(2)}) collective-permute-start(bf16[384,384]{1,0:T(8,128)(2,1)S(1)} %copy-done.21), channel_id=1, source_target_pairs={{0,6},{2,4},{4,2},{6,0},{8,14},{10,12},{12,10},{14,8},{16,22},{18,... | collective-permute-start | bytes 884744 | tf_op jit(solution)/shard_map/ppermute | solution.py:326
  246.2 6.4 %collective-permute-start.24 = (bf16[2,64,384]{2,1,0:T(8,128)(2,1)S(1)}, bf16[2,64,384]{2,1,0:T(8,128)(2,1)S(1)}, u32[]{:S(2)}, u32[]{:S(2)}) collective-permute-start(bf16[2,64,384]{2,1,0:T(8,128)(2,1)S(1)} %get-tuple-element.222), channel_id=1, source_target_pairs={{0,5},{1,4},{2,7},{3,6},{4,1},{5,0},{6,3},{7,2},{8,13},{9,12},{10,... | collective-permute-start | bytes 294920 | tf_op jit(solution)/shard_map/ppermute | solution.py:542
  247.8 6.4 %collective-permute-start.23 = (bf16[2,64,384]{2,1,0:T(8,128)(2,1)S(1)}, bf16[2,64,384]{2,1,0:T(8,128)(2,1)S(1)}, u32[]{:S(2)}, u32[]{:S(2)}) collective-permute-start(bf16[2,64,384]{2,1,0:T(8,128)(2,1)S(1)} %slice.214), channel_id=1, source_target_pairs={{0,4},{2,6},{4,0},{6,2},{8,12},{10,14},{12,8},{14,10},{16,20},{18,... | collective-permute-start | bytes 294920 | tf_op jit(solution)/shard_map/ppermute | solution.py:326
  254.3 10.2 %collective-permute-start.25 = (bf16[64,384]{1,0:T(8,128)(2,1)S(1)}, bf16[64,384]{1,0:T(8,128)(2,1)S(1)}, u32[]{:S(2)}, u32[]{:S(2)}) collective-permute-start(bf16[64,384]{1,0:T(8,128)(2,1)S(1)} %fusion.4), channel_id=1, source_target_pairs={{8,0},{10,2},{12,4},{14,6},{16,24},{18,26},{20,28},{22,30},{9,1},{... | collective-permute-start | bytes 147464 | tf_op jit(solution)/shard_map/ppermute | solution.py:323
  (29 other events, 196.3 us)
Sparse Core Ops, SparseCore 0:
  71.9 45.7 all-gather.6
  119.3 46.3 all-gather.8
  175.1 45.4 all-gather.10

commit v2 on v1

--- a/solution.py
+++ b/solution.py
@@ -87,7 +87,7 @@
     prev = [refs.pop(0) for _ in range(cfg["prev"])]
     outs = [refs.pop(0) for _ in range(cfg["n_outs"])]
     block_buffer, block_sem = refs.pop(0), refs.pop(0)
-    token_buffer, token_sem = refs.pop(0), refs.pop(0)
+    token_buffers = [(refs.pop(0), refs.pop(0)) for _ in groups]
     if held:
         held_buffer, held_sem = refs.pop(0), refs.pop(0)
     if final:
@@ -97,7 +97,7 @@
     core = idx[0]
     deep, width, rows = cfg["deep"], cfg["width"], cfg["rows"]
 
-    def token_copy(slot, unit, at):
+    def token_copy(buffer, sem, r, i, unit, at):
         g, d = unit
         ref, z = token_refs[cfg["tokens"][g][d]], idx[1 + cfg["planes"][at]]
         if len(ref.shape) == 2:
@@ -105,7 +105,11 @@
         else:
             start = pl.multiple_of((z % 2) * deep, deep)
             source = ref.at[2 * (core ^ (d & 1)) + z // 2, :, pl.ds(start, deep)]
-        return pltpu.make_async_copy(source, token_buffer.at[slot], token_sem.at[slot])
+        return pltpu.make_async_copy(source, buffer.at[r, :, pl.ds(i * deep, deep)], sem.at[r, i])
+
+    def block_copy(at):
+        target = block_buffer.at[pl.ds(at * deep, deep)]
+        return pltpu.make_async_copy(block_refs[at], target, block_sem.at[at])
 
     def arrived(buffer, sem, slot):
         pltpu.make_async_copy(buffer.at[slot], buffer.at[slot], sem.at[slot]).wait()
@@ -121,11 +125,10 @@
         source = ref.at[pl.ds(row, rows), pl.ds(column, width)]
         return pltpu.make_async_copy(source, grad_buffer.at[n], grad_sem.at[n])
 
-    def finish(group, r, n, both):
+    def finish(group, r, n, gate, up):
         s, d = group["units"][0]
         d = d + r
         arrived(grad_buffer, grad_sem, n)
-        gate, up = both[:, :width], both[:, width:]
         sig = 1.0 / (1.0 + jnp.exp(-gate))
         cotangent = grad_buffer[n].astype(jnp.float32)
         grad_gate = (cotangent * up * sig * (1.0 + gate * (1.0 - sig))).astype(jnp.bfloat16)
@@ -135,17 +138,14 @@
         outs[s][d] = prev[s][d] + part if s < len(prev) else part
 
     def work():
-        slot, n_kept, n, asked = 0, 0, 0, set()
-        for group in groups:
-            for unit in group["units"]:
-                for at in group["blocks"]:
+        n_kept, n, asked = 0, 0, set()
+        for group, (buffer, sem) in zip(groups, token_buffers):
+            for r, unit in enumerate(group["units"]):
+                for i, at in enumerate(group["blocks"]):
                     if at not in asked:
                         asked.add(at)
-                        pltpu.make_async_copy(
-                            block_refs[at], block_buffer.at[at], block_sem.at[at]
-                        ).start()
-                    token_copy(slot, unit, at).start()
-                    slot += 1
+                        block_copy(at).start()
+                    token_copy(buffer, sem, r, i, unit, at).start()
                 if group["held"]:
                     pltpu.make_async_copy(
                         kept[n_kept], held_buffer.at[n_kept], held_sem.at[n_kept]
@@ -154,48 +154,51 @@
                 if final:
                     grad_copy(n, unit).start()
                 n += 1
-        slot, n_kept, first, here = 0, 0, 0, set()
-        for group in groups:
+        n_kept, first, here = 0, 0, set()
+        for group, (buffer, sem) in zip(groups, token_buffers):
             size, count = len(group["blocks"]), len(group["units"])
             fresh = [at for at in group["blocks"] if at not in here]
             here.update(fresh)
+            planes = slice(group["blocks"][0] * deep, (group["blocks"][0] + size) * deep)
+            for at in fresh:
+                block_copy(at).wait()
 
             def unit_step(
-                r, carry, group=group, size=size, fresh=fresh, slot=slot, n_kept=n_kept, first=first
+                r, carry, group=group, buffer=buffer, sem=sem, planes=planes, n_kept=n_kept, first=first
             ):
-                both = None
-                for i, at in enumerate(group["blocks"]):
-                    if at in fresh:
-
-                        @pl.when(r == 0)
-                        def _(at=at):
-                            arrived(block_buffer, block_sem, at)
-
-                    arrived(token_buffer, token_sem, slot + r * size + i)
-                    term = jnp.dot(
-                        token_buffer[slot + r * size + i],
-                        block_buffer[at],
+                for i in range(buffer.shape[2] // deep):
+                    target = buffer.at[r, :, pl.ds(i * deep, deep)]
+                    pltpu.make_async_copy(target, target, sem.at[r, i]).wait()
+                pair = [
+                    jnp.dot(
+                        buffer[r],
+                        block_buffer[planes, h * width : (h + 1) * width],
                         preferred_element_type=jnp.float32,
                     )
-                    both = term if both is None else both + term
+                    for h in (0, 1)
+                ]
                 if group["held"]:
                     arrived(held_buffer, held_sem, n_kept + r)
-                    both = both + held_buffer[n_kept + r].astype(jnp.float32)
+                    pair = [
+                        value + held_buffer[n_kept + r, :, h * width : (h + 1) * width].astype(jnp.float32)
+                        for h, value in enumerate(pair)
+                    ]
                 n = first + r
                 if final:
-                    finish(group, r, n, both)
+                    finish(group, r, n, *pair)
                 else:
 
                     @pl.when(n >= 2)
                     def _():
                         out_copy(n - 2).wait()
 
-                    out_buffer[n % 2] = both.astype(out_buffer.dtype)
+                    for h, value in enumerate(pair):
+                        out_buffer[n % 2, :, h * width : (h + 1) * width] = value.astype(out_buffer.dtype)
                     out_copy(n).start()
                 return carry
 
             lax.fori_loop(0, count, unit_step, 0)
-            slot, first = slot + size * count, first + count
+            first += count
             if group["held"]:
                 n_kept += count
         if not final:
@@ -256,12 +259,17 @@
     else:
         results = [pltpu.HBM(shape, jnp.bfloat16) for shape in shapes]
 
-    def buffers(count, shape, dtype, first=rows):
-        return [pltpu.VMEM((count, first, shape), dtype), pltpu.SemaphoreType.DMA((count,))]
-
-    slots = sum(len(one["units"]) * len(one["blocks"]) for one in groups)
-    scratch = buffers(len(blocks), 2 * width, jnp.bfloat16, deep)
-    scratch += buffers(slots, deep, jnp.bfloat16)
+    def buffers(count, shape, dtype):
+        return [pltpu.VMEM((count, rows, shape), dtype), pltpu.SemaphoreType.DMA((count,))]
+
+    scratch = [
+        pltpu.VMEM((len(blocks) * deep, 2 * width), jnp.bfloat16),
+        pltpu.SemaphoreType.DMA((len(blocks),)),
+    ]
+    for one in groups:
+        units, size = len(one["units"]), len(one["blocks"])
+        scratch.append(pltpu.VMEM((units, rows, size * deep), jnp.bfloat16))
+        scratch.append(pltpu.SemaphoreType.DMA((units, size)))
     if held:
         scratch += buffers(sum(cfg["held"]), 2 * width, jnp.bfloat16)
     if final:

time: 274 us -> 272 us (level)
  waiting for transfers between devices: 147 us -> 143 us
    ppermute x11, waiting for transfers between devices: 51.3 us -> 47.8 us  [move(): return lax.ppermute(value, 'dp', perm)]
  transfers between devices with their start and end apart: 29 -> 29, of which waited for: 13 -> 13; matrix products, arithmetic and copies ran while one was open for 12% -> 12% of each run, Pallas kernels for 9% -> 10%
where the time goes in v2:
time: 272 us; the launch traced here: 271 us
  waiting for transfers between devices  143 us (53%)
  starting transfers between devices  43.4 us (16%)
  Pallas kernels  29.7 us (11%)
  local copies, waits for them, and re-layouts  20 us (7%)
  other arithmetic  17 us (6%)
  between operations  14.3 us (5%)
  matrix products  3.61 us (1%)
    ppermute x13, waiting for transfers between devices, flip(): return lax.ppermute(value, 'dp', [(i, i ^ d) for i in range(16)])  90.6 us
    ppermute x11, waiting for transfers between devices, move(): return lax.ppermute(value, 'dp', perm)  47.8 us
    ppermute x11, starting transfers between devices, move(): return lax.ppermute(value, 'dp', perm)  31.8 us
    pallas_call x7, Pallas kernels, ffn(): pl.pallas_call(functools.partial(ffn_kernel, cfg), out_shape=results, in_...  27.9 us
    ppermute x13, starting transfers between devices, flip(): return lax.ppermute(value, 'dp', [(i, i ^ d) for i in range(16)])  8.21 us
  transfers between devices with their start and end apart: 29, of which 13 were waited for; matrix products, arithmetic and copies ran while one was open for 12% of the time, Pallas kernels for 10%

profile of v2, /device:TPU:0, one launch (start us, length us, event | category | flops | bytes accessed | tf_op | source)
XLA Modules:
  0.0 271.5 jit_solution(12422384780806389517)
XLA Ops:
  7.3 2.7 constant_dynamic-slice_fusion.3
  10.0 2.2 constant_dynamic-slice_fusion.15
  14.2 2.8 %constant_dynamic-slice_fusion.19 = bf16[384,2048]{1,0:T(8,128)(2,1)} fusion(bf16[384,4096]{1,0:T(8,128)(2,1)} %refs_4_.3, s32[]{:T(128)S(6)} %select_n.134), kind=kLoop, calls=%fused_computation.74 | loop fusion | bytes 3145732 | tf_op jit(solution)/shard_map/dynamic_slice | solution.py:389
  20.8 1.9 collective-permute-start.3
  22.7 7.6 %collective-permute-start.4 = (bf16[384,2048]{1,0:T(8,128)(2,1)}, bf16[384,2048]{1,0:T(8,128)(2,1)}, u32[]{:S(2)}, u32[]{:S(2)}) collective-permute-start(bf16[384,2048]{1,0:T(8,128)(2,1)} %constant_dynamic-slice_fusion.19), channel_id=1, source_target_pairs={{0,8},{2,10},{4,12},{6,14},{24,16},{26,18},{28,20},{30,22},{1,9},{... | collective-permute-start | bytes 4718600 | tf_op jit(solution)/shard_map/ppermute | solution.py:331
  31.9 3.6 %fusion.9.projected = f32[64,384]{1,0:T(8,128)} fusion(bf16[64,4096]{1,0:T(8,128)(2,1)S(1)} %copy-done, bf16[384,4096]{1,0:T(8,128)(2,1)} %refs_4_.3), kind=kOutput, calls=%fused_computation.83 | convolution fusion | flops 201326592 | bytes 3768320 | tf_op jit(solution)/shard_map/dot_general | solution.py:17
  35.5 18.1 %collective-permute-done.1 = bf16[256,1792]{1,0:T(8,128)(2,1)S(1)} collective-permute-done((bf16[256,1792]{1,0:T(8,128)(2,1)S(1)}, bf16[256,1792]{1,0:T(8,128)(2,1)S(1)}, u32[]{:S(2)}, u32[]{:S(2)}) %collective-permute-start.1) | collective-permute-done | bytes 917536 | tf_op jit(solution)/shard_map/ppermute | solution.py:334
  53.6 17.2 %collective-permute-done.2 = bf16[256,1792]{1,0:T(8,128)(2,1)S(1)} collective-permute-done((bf16[256,1792]{1,0:T(8,128)(2,1)S(1)}, bf16[256,1792]{1,0:T(8,128)(2,1)S(1)}, u32[]{:S(2)}, u32[]{:S(2)}) %collective-permute-start.2) | collective-permute-done | bytes 917536 | tf_op jit(solution)/shard_map/ppermute | solution.py:334
  75.0 1.9 collective-permute-start.6
  82.9 1.9 constant_dynamic-slice_fusion.1
  87.9 28.0 %collective-permute-done.7.refs_1_ = bf16[1024,768]{1,0:T(8,128)(2,1)} collective-permute-done((bf16[1024,768]{1,0:T(8,128)(2,1)}, bf16[1024,768]{1,0:T(8,128)(2,1)}, u32[]{:S(2)}, u32[]{:S(2)}) %collective-permute-start.7) | collective-permute-done | bytes 1572896 | tf_op jit(solution)/shard_map/ppermute | solution.py:331
  116.0 5.8 %collective-permute-start.13 = (bf16[1024,1024]{1,0:T(8,128)(2,1)S(1)}, bf16[1024,1024]{1,0:T(8,128)(2,1)}, u32[]{:S(2)}, u32[]{:S(2)}) collective-permute-start(bf16[1024,1024]{1,0:T(8,128)(2,1)S(1)} %pad_maximum_fusion.2.refs_0_), channel_id=1, source_target_pairs={{0,8},{2,10},{4,12},{6,14},{24,16},{26,18},{28,20},{30,22},{1,9},{... | collective-permute-start | bytes 6291464 | tf_op jit(solution)/shard_map/ppermute | solution.py:331
  134.3 40.6 %collective-permute-done.11 = bf16[2,384,512]{2,1,0:T(8,128)(2,1)} collective-permute-done((bf16[2,384,512]{2,1,0:T(8,128)(2,1)S(1)}, bf16[2,384,512]{2,1,0:T(8,128)(2,1)}, u32[]{:S(2)}, u32[]{:S(2)}) %collective-permute-start.11) | collective-permute-done | bytes 786464 | tf_op jit(solution)/shard_map/ppermute | solution.py:334
  176.3 2.0 collective-permute-start.20
  180.9 6.8 %collective-permute-start.19 = (bf16[1536,512]{1,0:T(8,128)(2,1)S(1)}, bf16[1536,512]{1,0:T(8,128)(2,1)}, u32[]{:S(2)}, u32[]{:S(2)}) collective-permute-start(bf16[1536,512]{1,0:T(8,128)(2,1)S(1)} %pad_maximum_fusion.6.refs_10_.refs_11_.refs_12_.refs_13_), channel_id=1, source_target_pairs={{0,8},{2,10},{4,12},{6,14},{24,16},{26,18},{28,20},{30,22},{1,9},{... | collective-permute-start | bytes 4718600 | tf_op jit(solution)/shard_map/ppermute | solution.py:331
  190.9 6.7 %collective-permute-done.15.refs_8_ = bf16[384,384]{1,0:T(8,128)(2,1)S(1)} collective-permute-done((bf16[384,384]{1,0:T(8,128)(2,1)S(1)}, bf16[384,384]{1,0:T(8,128)(2,1)S(1)}, u32[]{:S(2)}, u32[]{:S(2)}) %collective-permute-start.15) | collective-permute-done | bytes 294944 | tf_op jit(solution)/shard_map/ppermute | solution.py:334
  197.6 4.4 %collective-permute-done.16.refs_9_ = bf16[384,384]{1,0:T(8,128)(2,1)S(1)} collective-permute-done((bf16[384,384]{1,0:T(8,128)(2,1)S(1)}, bf16[384,384]{1,0:T(8,128)(2,1)S(1)}, u32[]{:S(2)}, u32[]{:S(2)}) %collective-permute-start.16) | collective-permute-done | bytes 294944 | tf_op jit(solution)/shard_map/ppermute | solution.py:334
  203.5 15.0 %collective-permute-done.17 = bf16[1024,768]{1,0:T(8,128)(2,1)} collective-permute-done((bf16[1024,768]{1,0:T(8,128)(2,1)}, bf16[1024,768]{1,0:T(8,128)(2,1)}, u32[]{:S(2)}, u32[]{:S(2)}) %collective-permute-start.17) | collective-permute-done | bytes 1572896 | tf_op jit(solution)/shard_map/ppermute | solution.py:331
  218.5 2.1 all-gather.11.cloned.1.call-done
  220.6 23.2 %conditional.1 = (f32[4,128,384]{2,1,0:T(8,128)S(1)}) conditional(s32[]{:T(128)} %convert_element_type.24, (s32[6]{0:T(128)S(1)}, bf16[1024,768]{1,0:T(8,128)(2,1)}, bf16[1024,768]{1,0:T(8,128)(2,1)}, bf16[1024,768]{1,0:T(8,128)(2,1)}, bf16[1024,768]{1,0:T(8,128)(2,1)}, /*index=5*/bf16[384,4096]{1,0:T(8,128)(2,1)}, bf16[384,4096]{1,0:T(8,128)(2,1)}, ...), branch_computations={%region_0.1_spmd, %region_1.2_spmd} | conditional | flops 1 | bytes 1572873 | solution.py:521
  220.6 23.2 %a_end.1 = f32[4,128,384]{2,1,0:T(8,128)S(1)} custom-call(s32[6]{0:T(128)S(1)} %get-tuple-element.34.idx, bf16[1024,768]{1,0:T(8,128)(2,1)} %get-tuple-element.35.refs_0_, bf16[1024,768]{1,0:T(8,128)(2,1)} %get-tuple-element.36.refs_1_, bf16[1024,768]{1,0:T(8,128)(2,1)} %get-tuple-element.37.refs_2_, bf16[1024,768]{1,0:T(8,128)(2,1)} %get-tuple-element.38.refs_3_, ...), custom_call_target="tpu_custom_call" | custom-call | flops 1 | bytes 1 | tf_op jit(solution)/shard_map/cond/branch_0_fun/a_end/pallas_call | solution.py:279
  245.5 2.0 collective-permute-done.21
  251.4 2.7 %collective-permute-done.24 = bf16[2,64,384]{2,1,0:T(8,128)(2,1)S(1)} collective-permute-done((bf16[2,64,384]{2,1,0:T(8,128)(2,1)S(1)}, bf16[2,64,384]{2,1,0:T(8,128)(2,1)S(1)}, u32[]{:S(2)}, u32[]{:S(2)}) %collective-permute-start.24) | collective-permute-done | bytes 98336 | tf_op jit(solution)/shard_map/ppermute | solution.py:550
  257.8 4.7 %collective-permute-done.25.sent = bf16[64,384]{1,0:T(8,128)(2,1)S(1)} collective-permute-done((bf16[64,384]{1,0:T(8,128)(2,1)S(1)}, bf16[64,384]{1,0:T(8,128)(2,1)S(1)}, u32[]{:S(2)}, u32[]{:S(2)}) %collective-permute-start.25) | collective-permute-done | bytes 49184 | tf_op jit(solution)/shard_map/ppermute | solution.py:331
  (138 shorter events, 53.1 us)
Async XLA Ops:
  7.2 126.5 %all-gather.7.cloned.1.call-start = ((), (), s32[]{:S(2)}) async-start(), calls=%async_computation | async-start | bytes 7864320 | tf_op jit(solution)/shard_map/all_gather | solution.py:341
  12.7 59.1 %collective-permute-start.5 = (bf16[384,4096]{1,0:T(8,128)(2,1)}, bf16[384,4096]{1,0:T(8,128)(2,1)}, u32[]{:S(2)}, u32[]{:S(2)}) collective-permute-start(bf16[384,4096]{1,0:T(8,128)(2,1)} %refs_4_.3), channel_id=1, source_target_pairs={{0,2},{2,0},{4,6},{6,4},{8,10},{10,8},{12,14},{14,12},{16,18},{18,... | collective-permute-start | bytes 9437192 | tf_op jit(solution)/shard_map/ppermute | solution.py:334
  20.8 51.0 %collective-permute-start.3 = (bf16[512,1792]{1,0:T(8,128)(2,1)}, bf16[512,1792]{1,0:T(8,128)(2,1)}, u32[]{:S(2)}, u32[]{:S(2)}) collective-permute-start(bf16[512,1792]{1,0:T(8,128)(2,1)} %pad_maximum_fusion), channel_id=1, source_target_pairs={{8,16},{10,18},{12,20},{14,22},{16,8},{18,10},{20,12},{22,14},{9,1... | collective-permute-start | bytes 5505032 | tf_op jit(solution)/shard_map/ppermute | solution.py:331
  22.7 49.0 %collective-permute-start.4 = (bf16[384,2048]{1,0:T(8,128)(2,1)}, bf16[384,2048]{1,0:T(8,128)(2,1)}, u32[]{:S(2)}, u32[]{:S(2)}) collective-permute-start(bf16[384,2048]{1,0:T(8,128)(2,1)} %constant_dynamic-slice_fusion.19), channel_id=1, source_target_pairs={{0,8},{2,10},{4,12},{6,14},{24,16},{26,18},{28,20},{30,22},{1,9},{... | collective-permute-start | bytes 4718600 | tf_op jit(solution)/shard_map/ppermute | solution.py:331
  30.4 23.3 %collective-permute-start.1 = (bf16[256,1792]{1,0:T(8,128)(2,1)S(1)}, bf16[256,1792]{1,0:T(8,128)(2,1)S(1)}, u32[]{:S(2)}, u32[]{:S(2)}) collective-permute-start(bf16[256,1792]{1,0:T(8,128)(2,1)S(1)} %pad_maximum_fusion.7), channel_id=1, source_target_pairs={{0,4},{2,6},{4,0},{6,2},{8,12},{10,14},{12,8},{14,10},{16,20},{18,... | collective-permute-start | bytes 2752520 | tf_op jit(solution)/shard_map/ppermute | solution.py:334
  31.9 39.0 %collective-permute-start.2 = (bf16[256,1792]{1,0:T(8,128)(2,1)S(1)}, bf16[256,1792]{1,0:T(8,128)(2,1)S(1)}, u32[]{:S(2)}, u32[]{:S(2)}) collective-permute-start(bf16[256,1792]{1,0:T(8,128)(2,1)S(1)} %pad_maximum_fusion.8), channel_id=1, source_target_pairs={{0,6},{2,4},{4,2},{6,0},{8,14},{10,12},{12,10},{14,8},{16,22},{18,... | collective-permute-start | bytes 2752520 | tf_op jit(solution)/shard_map/ppermute | solution.py:334
  71.8 103.1 %all-gather.9.cloned.1.call-start = ((), (), s32[]{:S(2)}) async-start(), calls=%async_computation.1 | async-start | bytes 7864320 | tf_op jit(solution)/shard_map/all_gather | solution.py:341
  75.0 40.9 %collective-permute-start.6 = (bf16[512,1792]{1,0:T(8,128)(2,1)}, bf16[512,1792]{1,0:T(8,128)(2,1)}, u32[]{:S(2)}, u32[]{:S(2)}) collective-permute-start(bf16[512,1792]{1,0:T(8,128)(2,1)} %pad_maximum_fusion.1), channel_id=1, source_target_pairs={{8,16},{10,18},{12,20},{14,22},{16,8},{18,10},{20,12},{22,14},{9,1... | collective-permute-start | bytes 5505032 | tf_op jit(solution)/shard_map/ppermute | solution.py:331
  78.5 37.4 %collective-permute-start.7 = (bf16[1024,768]{1,0:T(8,128)(2,1)}, bf16[1024,768]{1,0:T(8,128)(2,1)}, u32[]{:S(2)}, u32[]{:S(2)}) collective-permute-start(bf16[1024,768]{1,0:T(8,128)(2,1)} %pad_maximum_fusion.4.refs_0_), channel_id=1, source_target_pairs={{0,8},{2,10},{4,12},{6,14},{8,0},{10,2},{12,4},{14,6},{16,24},{18,... | collective-permute-start | bytes 4718600 | tf_op jit(solution)/shard_map/ppermute | solution.py:331
  78.5 37.4 %collective-permute-start.8 = (bf16[384,2048]{1,0:T(8,128)(2,1)}, bf16[384,2048]{1,0:T(8,128)(2,1)}, u32[]{:S(2)}, u32[]{:S(2)}) collective-permute-start(bf16[384,2048]{1,0:T(8,128)(2,1)} %constant_dynamic-slice_fusion.19), channel_id=1, source_target_pairs={{0,4},{2,6},{4,0},{6,2},{8,12},{10,14},{12,8},{14,10},{16,20},{18,... | collective-permute-start | bytes 4718600 | tf_op jit(solution)/shard_map/ppermute | solution.py:334
  115.9 104.7 %all-gather.11.cloned.1.call-start = ((), (), s32[]{:S(2)}) async-start(), calls=%async_computation.2 | async-start | bytes 7864320 | tf_op jit(solution)/shard_map/all_gather | solution.py:341
  116.0 58.9 %collective-permute-start.13 = (bf16[1024,1024]{1,0:T(8,128)(2,1)S(1)}, bf16[1024,1024]{1,0:T(8,128)(2,1)}, u32[]{:S(2)}, u32[]{:S(2)}) collective-permute-start(bf16[1024,1024]{1,0:T(8,128)(2,1)S(1)} %pad_maximum_fusion.2.refs_0_), channel_id=1, source_target_pairs={{0,8},{2,10},{4,12},{6,14},{24,16},{26,18},{28,20},{30,22},{1,9},{... | collective-permute-start | bytes 6291464 | tf_op jit(solution)/shard_map/ppermute | solution.py:331
  121.8 53.1 %collective-permute-start.10 = (bf16[384,2048]{1,0:T(8,128)(2,1)}, bf16[384,2048]{1,0:T(8,128)(2,1)}, u32[]{:S(2)}, u32[]{:S(2)}) collective-permute-start(bf16[384,2048]{1,0:T(8,128)(2,1)} %collective-permute-done.4), channel_id=1, source_target_pairs={{0,4},{2,6},{4,0},{6,2},{8,12},{10,14},{12,8},{14,10},{16,20},{18,... | collective-permute-start | bytes 4718600 | tf_op jit(solution)/shard_map/ppermute | solution.py:334
  123.2 51.7 %collective-permute-start.12 = (bf16[1024,768]{1,0:T(8,128)(2,1)}, bf16[1024,768]{1,0:T(8,128)(2,1)}, u32[]{:S(2)}, u32[]{:S(2)}) collective-permute-start(bf16[1024,768]{1,0:T(8,128)(2,1)} %collective-permute-done.7.refs_1_), channel_id=1, source_target_pairs={{8,16},{10,18},{12,20},{14,22},{16,8},{18,10},{20,12},{22,14},{9,1... | collective-permute-start | bytes 4718600 | tf_op jit(solution)/shard_map/ppermute | solution.py:331
  127.9 46.9 %collective-permute-start.14 = (bf16[1024,768]{1,0:T(8,128)(2,1)}, bf16[1024,768]{1,0:T(8,128)(2,1)}, u32[]{:S(2)}, u32[]{:S(2)}) collective-permute-start(bf16[1024,768]{1,0:T(8,128)(2,1)} %pad_maximum_fusion.5.refs_2_), channel_id=1, source_target_pairs={{8,0},{10,2},{12,4},{14,6},{16,24},{18,26},{20,28},{22,30},{9,1},{... | collective-permute-start | bytes 4718600 | tf_op jit(solution)/shard_map/ppermute | solution.py:331
  129.2 45.6 %collective-permute-start.11 = (bf16[2,384,512]{2,1,0:T(8,128)(2,1)S(1)}, bf16[2,384,512]{2,1,0:T(8,128)(2,1)}, u32[]{:S(2)}, u32[]{:S(2)}) collective-permute-start(bf16[2,384,512]{2,1,0:T(8,128)(2,1)S(1)} %copy-done.16), channel_id=1, source_target_pairs={{0,4},{2,6},{4,0},{6,2},{8,12},{10,14},{12,8},{14,10},{16,20},{18,... | collective-permute-start | bytes 2359304 | tf_op jit(solution)/shard_map/ppermute | solution.py:334
  176.3 67.6 %collective-permute-start.20 = (bf16[1024,1024]{1,0:T(8,128)(2,1)}, bf16[1024,1024]{1,0:T(8,128)(2,1)}, u32[]{:S(2)}, u32[]{:S(2)}) collective-permute-start(bf16[1024,1024]{1,0:T(8,128)(2,1)} %collective-permute-done.13.refs_1_), channel_id=1, source_target_pairs={{8,16},{10,18},{12,20},{14,22},{16,8},{18,10},{20,12},{22,14},{9,1... | collective-permute-start | bytes 6291464 | tf_op jit(solution)/shard_map/ppermute | solution.py:331
  179.3 39.1 %collective-permute-start.17 = (bf16[1024,768]{1,0:T(8,128)(2,1)}, bf16[1024,768]{1,0:T(8,128)(2,1)}, u32[]{:S(2)}, u32[]{:S(2)}) collective-permute-start(bf16[1024,768]{1,0:T(8,128)(2,1)} %collective-permute-done.12.refs_0_), channel_id=1, source_target_pairs={{8,0},{10,2},{12,4},{14,6},{16,24},{18,26},{20,28},{22,30},{9,1},{... | collective-permute-start | bytes 4718600 | tf_op jit(solution)/shard_map/ppermute | solution.py:331
  180.9 62.9 %collective-permute-start.19 = (bf16[1536,512]{1,0:T(8,128)(2,1)S(1)}, bf16[1536,512]{1,0:T(8,128)(2,1)}, u32[]{:S(2)}, u32[]{:S(2)}) collective-permute-start(bf16[1536,512]{1,0:T(8,128)(2,1)S(1)} %pad_maximum_fusion.6.refs_10_.refs_11_.refs_12_.refs_13_), channel_id=1, source_target_pairs={{0,8},{2,10},{4,12},{6,14},{24,16},{26,18},{28,20},{30,22},{1,9},{... | collective-permute-start | bytes 4718600 | tf_op jit(solution)/shard_map/ppermute | solution.py:331
  187.7 9.9 %collective-permute-start.15 = (bf16[384,384]{1,0:T(8,128)(2,1)S(1)}, bf16[384,384]{1,0:T(8,128)(2,1)S(1)}, u32[]{:S(2)}, u32[]{:S(2)}) collective-permute-start(bf16[384,384]{1,0:T(8,128)(2,1)S(1)} %copy-done.22), channel_id=1, source_target_pairs={{0,4},{2,6},{4,0},{6,2},{8,12},{10,14},{12,8},{14,10},{16,20},{18,... | collective-permute-start | bytes 884744 | tf_op jit(solution)/shard_map/ppermute | solution.py:334
  189.3 12.7 %collective-permute-start.16 = (bf16[384,384]{1,0:T(8,128)(2,1)S(1)}, bf16[384,384]{1,0:T(8,128)(2,1)S(1)}, u32[]{:S(2)}, u32[]{:S(2)}) collective-permute-start(bf16[384,384]{1,0:T(8,128)(2,1)S(1)} %copy-done.21), channel_id=1, source_target_pairs={{0,6},{2,4},{4,2},{6,0},{8,14},{10,12},{12,10},{14,8},{16,22},{18,... | collective-permute-start | bytes 884744 | tf_op jit(solution)/shard_map/ppermute | solution.py:334
  247.7 6.4 %collective-permute-start.24 = (bf16[2,64,384]{2,1,0:T(8,128)(2,1)S(1)}, bf16[2,64,384]{2,1,0:T(8,128)(2,1)S(1)}, u32[]{:S(2)}, u32[]{:S(2)}) collective-permute-start(bf16[2,64,384]{2,1,0:T(8,128)(2,1)S(1)} %get-tuple-element.222), channel_id=1, source_target_pairs={{0,5},{1,4},{2,7},{3,6},{4,1},{5,0},{6,3},{7,2},{8,13},{9,12},{10,... | collective-permute-start | bytes 294920 | tf_op jit(solution)/shard_map/ppermute | solution.py:550
  249.3 6.4 %collective-permute-start.23 = (bf16[2,64,384]{2,1,0:T(8,128)(2,1)S(1)}, bf16[2,64,384]{2,1,0:T(8,128)(2,1)S(1)}, u32[]{:S(2)}, u32[]{:S(2)}) collective-permute-start(bf16[2,64,384]{2,1,0:T(8,128)(2,1)S(1)} %slice.214), channel_id=1, source_target_pairs={{0,4},{2,6},{4,0},{6,2},{8,12},{10,14},{12,8},{14,10},{16,20},{18,... | collective-permute-start | bytes 294920 | tf_op jit(solution)/shard_map/ppermute | solution.py:334
  255.9 6.7 %collective-permute-start.25 = (bf16[64,384]{1,0:T(8,128)(2,1)S(1)}, bf16[64,384]{1,0:T(8,128)(2,1)S(1)}, u32[]{:S(2)}, u32[]{:S(2)}) collective-permute-start(bf16[64,384]{1,0:T(8,128)(2,1)S(1)} %fusion.4), channel_id=1, source_target_pairs={{8,0},{10,2},{12,4},{14,6},{16,24},{18,26},{20,28},{22,30},{9,1},{... | collective-permute-start | bytes 147464 | tf_op jit(solution)/shard_map/ppermute | solution.py:331
  (29 other events, 192.6 us)
Sparse Core Ops, SparseCore 0:
  71.9 45.7 all-gather.6
  119.3 46.3 all-gather.8
  175.1 45.4 all-gather.10

commit v3 on v2

--- a/solution.py
+++ b/solution.py
@@ -358,9 +358,10 @@
     def quarter_of(value, d):
         return lax.dynamic_slice_in_dim(value, (q ^ d) * quarter, quarter, 1)
 
-    def weights_for(d, chunk):
-        gate, up = quarter_of(gate_weight, d), quarter_of(up_weight, d)
-        return jnp.concatenate([gate[:, chunk], up[:, chunk]], axis=1)
+    def weights_for(d, whole_gate, whole_up):
+        gate, up = quarter_of(whole_gate, d), quarter_of(whole_up, d)
+        pieces = [value[:, chunk] for chunk in (chunk_a, chunk_b) for value in (gate, up)]
+        return jnp.concatenate(pieces, axis=1)
 
     def grads_for(d, chunk):
         return quarter_of(hidden_grad, d)[:, chunk]
@@ -383,12 +384,13 @@
     proj_b = [gate_rows[:, chunk_b], up_rows[:, chunk_b]]
 
     wide_a, wide_b = slice(0, 2 * cut), slice(2 * cut, 2 * quarter)
-    both = [
-        jnp.concatenate([weights_for(d, chunk_a), weights_for(d, chunk_b)], axis=1) for d in range(4)
-    ]
+    to_core = weights_for(1, gate_weight, up_weight)
+    weights = lax.optimization_barrier((gate_weight, up_weight, to_core))
+    both = [None if d == 1 else weights_for(d, *weights[:2]) for d in range(4)]
+    both[1] = weights[2]
     half = lax.dynamic_slice_in_dim(tokens, x * (model // 2), model // 2, 1)
     core_in = flip(both[1], 1)
-    both[2], both[3], half, core_in = wait(both[2], both[3], half, core_in)
+    half, core_in = wait(half, core_in)
     side_in, cross_in = flip(both[2], 2), flip(both[3], 3)
     end_half = move(half, inward)
     u0 = by_core(both[0], core_in)

time: 272 us -> 269 us (0.989)
  transfers between devices with their start and end apart: 29 -> 29, of which waited for: 13 -> 13; matrix products, arithmetic and copies ran while one was open for 12% -> 11% of each run, Pallas kernels for 10% -> 10%
where the time goes in v3:
time: 269 us; the launch traced here: 268 us
  waiting for transfers between devices  143 us (53%)
  starting transfers between devices  43.5 us (16%)
  Pallas kernels  29.7 us (11%)
  local copies, waits for them, and re-layouts  18 us (7%)
  other arithmetic  16 us (6%)
  between operations  14.3 us (5%)
  matrix products  3.62 us (1%)
    ppermute x13, waiting for transfers between devices, flip(): return lax.ppermute(value, 'dp', [(i, i ^ d) for i in range(16)])  90.5 us
    ppermute x11, waiting for transfers between devices, move(): return lax.ppermute(value, 'dp', perm)  47.7 us
    ppermute x11, starting transfers between devices, move(): return lax.ppermute(value, 'dp', perm)  31.8 us
    pallas_call x7, Pallas kernels, ffn(): pl.pallas_call(functools.partial(ffn_kernel, cfg), out_shape=results, in_...  27.9 us
    ppermute x13, starting transfers between devices, flip(): return lax.ppermute(value, 'dp', [(i, i ^ d) for i in range(16)])  8.34 us
  transfers between devices with their start and end apart: 29, of which 13 were waited for; matrix products, arithmetic and copies ran while one was open for 11% of the time, Pallas kernels for 10%

profile of v3, /device:TPU:0, one launch (start us, length us, event | category | flops | bytes accessed | tf_op | source)
XLA Modules:
  0.0 268.4 jit_solution(14463567658554309799)
XLA Ops:
  12.0 2.7 %constant_dynamic-slice_fusion.15 = bf16[384,2048]{1,0:T(8,128)(2,1)} fusion(bf16[384,4096]{1,0:T(8,128)(2,1)} %refs_4_.3, s32[]{:T(128)S(6)} %select_n.128), kind=kLoop, calls=%fused_computation.70 | loop fusion | bytes 3145732 | tf_op jit(solution)/shard_map/dynamic_slice | solution.py:391
  17.6 1.9 collective-permute-start.3
  19.5 7.6 %collective-permute-start.4 = (bf16[384,2048]{1,0:T(8,128)(2,1)}, bf16[384,2048]{1,0:T(8,128)(2,1)}, u32[]{:S(2)}, u32[]{:S(2)}) collective-permute-start(bf16[384,2048]{1,0:T(8,128)(2,1)} %constant_dynamic-slice_fusion.15), channel_id=1, source_target_pairs={{0,8},{2,10},{4,12},{6,14},{24,16},{26,18},{28,20},{30,22},{1,9},{... | collective-permute-start | bytes 4718600 | tf_op jit(solution)/shard_map/ppermute | solution.py:331
  28.9 3.6 %fusion.9.projected = f32[64,384]{1,0:T(8,128)} fusion(bf16[64,4096]{1,0:T(8,128)(2,1)S(1)} %copy-done, bf16[384,4096]{1,0:T(8,128)(2,1)} %refs_4_.3), kind=kOutput, calls=%fused_computation.83 | convolution fusion | flops 201326592 | bytes 3768320 | tf_op jit(solution)/shard_map/dot_general | solution.py:17
  32.6 18.0 %collective-permute-done = bf16[256,1792]{1,0:T(8,128)(2,1)S(1)} collective-permute-done((bf16[256,1792]{1,0:T(8,128)(2,1)S(1)}, bf16[256,1792]{1,0:T(8,128)(2,1)S(1)}, u32[]{:S(2)}, u32[]{:S(2)}) %collective-permute-start) | collective-permute-done | bytes 917536 | tf_op jit(solution)/shard_map/ppermute | solution.py:334
  50.6 17.2 %collective-permute-done.1 = bf16[256,1792]{1,0:T(8,128)(2,1)S(1)} collective-permute-done((bf16[256,1792]{1,0:T(8,128)(2,1)S(1)}, bf16[256,1792]{1,0:T(8,128)(2,1)S(1)}, u32[]{:S(2)}, u32[]{:S(2)}) %collective-permute-start.1) | collective-permute-done | bytes 917536 | tf_op jit(solution)/shard_map/ppermute | solution.py:334
  71.9 1.9 collective-permute-start.6
  79.9 1.9 constant_dynamic-slice_fusion.1
  84.8 28.0 %collective-permute-done.7.refs_1_ = bf16[1024,768]{1,0:T(8,128)(2,1)} collective-permute-done((bf16[1024,768]{1,0:T(8,128)(2,1)}, bf16[1024,768]{1,0:T(8,128)(2,1)}, u32[]{:S(2)}, u32[]{:S(2)}) %collective-permute-start.7) | collective-permute-done | bytes 1572896 | tf_op jit(solution)/shard_map/ppermute | solution.py:331
  112.9 5.7 %collective-permute-start.13 = (bf16[1024,1024]{1,0:T(8,128)(2,1)S(1)}, bf16[1024,1024]{1,0:T(8,128)(2,1)}, u32[]{:S(2)}, u32[]{:S(2)}) collective-permute-start(bf16[1024,1024]{1,0:T(8,128)(2,1)S(1)} %pad_maximum_fusion.2.refs_0_), channel_id=1, source_target_pairs={{0,8},{2,10},{4,12},{6,14},{24,16},{26,18},{28,20},{30,22},{1,9},{... | collective-permute-start | bytes 6291464 | tf_op jit(solution)/shard_map/ppermute | solution.py:331
  120.0 1.8 collective-permute-start.12
  131.1 40.6 %collective-permute-done.11 = bf16[2,384,512]{2,1,0:T(8,128)(2,1)} collective-permute-done((bf16[2,384,512]{2,1,0:T(8,128)(2,1)S(1)}, bf16[2,384,512]{2,1,0:T(8,128)(2,1)}, u32[]{:S(2)}, u32[]{:S(2)}) %collective-permute-start.11) | collective-permute-done | bytes 786464 | tf_op jit(solution)/shard_map/ppermute | solution.py:334
  173.1 2.0 collective-permute-start.20
  177.8 6.9 %collective-permute-start.19 = (bf16[1536,512]{1,0:T(8,128)(2,1)S(1)}, bf16[1536,512]{1,0:T(8,128)(2,1)}, u32[]{:S(2)}, u32[]{:S(2)}) collective-permute-start(bf16[1536,512]{1,0:T(8,128)(2,1)S(1)} %pad_maximum_fusion.6.refs_10_.refs_11_.refs_12_.refs_13_), channel_id=1, source_target_pairs={{0,8},{2,10},{4,12},{6,14},{24,16},{26,18},{28,20},{30,22},{1,9},{... | collective-permute-start | bytes 4718600 | tf_op jit(solution)/shard_map/ppermute | solution.py:331
  187.8 6.7 %collective-permute-done.15.refs_8_ = bf16[384,384]{1,0:T(8,128)(2,1)S(1)} collective-permute-done((bf16[384,384]{1,0:T(8,128)(2,1)S(1)}, bf16[384,384]{1,0:T(8,128)(2,1)S(1)}, u32[]{:S(2)}, u32[]{:S(2)}) %collective-permute-start.15) | collective-permute-done | bytes 294944 | tf_op jit(solution)/shard_map/ppermute | solution.py:334
  194.5 4.4 %collective-permute-done.16.refs_9_ = bf16[384,384]{1,0:T(8,128)(2,1)S(1)} collective-permute-done((bf16[384,384]{1,0:T(8,128)(2,1)S(1)}, bf16[384,384]{1,0:T(8,128)(2,1)S(1)}, u32[]{:S(2)}, u32[]{:S(2)}) %collective-permute-start.16) | collective-permute-done | bytes 294944 | tf_op jit(solution)/shard_map/ppermute | solution.py:334
  200.3 15.0 %collective-permute-done.17 = bf16[1024,768]{1,0:T(8,128)(2,1)} collective-permute-done((bf16[1024,768]{1,0:T(8,128)(2,1)}, bf16[1024,768]{1,0:T(8,128)(2,1)}, u32[]{:S(2)}, u32[]{:S(2)}) %collective-permute-start.17) | collective-permute-done | bytes 1572896 | tf_op jit(solution)/shard_map/ppermute | solution.py:331
  215.3 2.1 all-gather.11.cloned.1.call-done
  217.4 23.2 %conditional.1 = (f32[4,128,384]{2,1,0:T(8,128)S(1)}) conditional(s32[]{:T(128)} %convert_element_type.24, (s32[6]{0:T(128)S(1)}, bf16[1024,768]{1,0:T(8,128)(2,1)}, bf16[1024,768]{1,0:T(8,128)(2,1)}, bf16[1024,768]{1,0:T(8,128)(2,1)}, bf16[1024,768]{1,0:T(8,128)(2,1)}, /*index=5*/bf16[384,4096]{1,0:T(8,128)(2,1)}, bf16[384,4096]{1,0:T(8,128)(2,1)}, ...), branch_computations={%region_0.1_spmd, %region_1.2_spmd} | conditional | flops 1 | bytes 1572873 | solution.py:523
  217.5 23.2 %a_end.1 = f32[4,128,384]{2,1,0:T(8,128)S(1)} custom-call(s32[6]{0:T(128)S(1)} %get-tuple-element.34.idx, bf16[1024,768]{1,0:T(8,128)(2,1)} %get-tuple-element.35.refs_0_, bf16[1024,768]{1,0:T(8,128)(2,1)} %get-tuple-element.36.refs_1_, bf16[1024,768]{1,0:T(8,128)(2,1)} %get-tuple-element.37.refs_2_, bf16[1024,768]{1,0:T(8,128)(2,1)} %get-tuple-element.38.refs_3_, ...), custom_call_target="tpu_custom_call" | custom-call | flops 1 | bytes 1 | tf_op jit(solution)/shard_map/cond/branch_0_fun/a_end/pallas_call | solution.py:279
  242.4 2.0 collective-permute-done.21
  248.3 2.7 %collective-permute-done.24 = bf16[2,64,384]{2,1,0:T(8,128)(2,1)S(1)} collective-permute-done((bf16[2,64,384]{2,1,0:T(8,128)(2,1)S(1)}, bf16[2,64,384]{2,1,0:T(8,128)(2,1)S(1)}, u32[]{:S(2)}, u32[]{:S(2)}) %collective-permute-start.24) | collective-permute-done | bytes 98336 | tf_op jit(solution)/shard_map/ppermute | solution.py:552
  254.7 4.8 %collective-permute-done.25.sent = bf16[64,384]{1,0:T(8,128)(2,1)S(1)} collective-permute-done((bf16[64,384]{1,0:T(8,128)(2,1)S(1)}, bf16[64,384]{1,0:T(8,128)(2,1)S(1)}, u32[]{:S(2)}, u32[]{:S(2)}) %collective-permute-start.25) | collective-permute-done | bytes 49184 | tf_op jit(solution)/shard_map/ppermute | solution.py:331
  260.0 1.8 features.1
  (130 shorter events, 51.6 us)
Async XLA Ops:
  7.2 123.3 %all-gather.7.cloned.1.call-start = ((), (), s32[]{:S(2)}) async-start(), calls=%async_computation | async-start | bytes 7864320 | tf_op jit(solution)/shard_map/all_gather | solution.py:341
  10.2 58.5 %collective-permute-start.5 = (bf16[384,4096]{1,0:T(8,128)(2,1)}, bf16[384,4096]{1,0:T(8,128)(2,1)}, u32[]{:S(2)}, u32[]{:S(2)}) collective-permute-start(bf16[384,4096]{1,0:T(8,128)(2,1)} %refs_4_.3), channel_id=1, source_target_pairs={{0,2},{2,0},{4,6},{6,4},{8,10},{10,8},{12,14},{14,12},{16,18},{18,... | collective-permute-start | bytes 9437192 | tf_op jit(solution)/shard_map/ppermute | solution.py:334
  17.6 51.1 %collective-permute-start.3 = (bf16[512,1792]{1,0:T(8,128)(2,1)}, bf16[512,1792]{1,0:T(8,128)(2,1)}, u32[]{:S(2)}, u32[]{:S(2)}) collective-permute-start(bf16[512,1792]{1,0:T(8,128)(2,1)} %pad_maximum_fusion), channel_id=1, source_target_pairs={{8,16},{10,18},{12,20},{14,22},{16,8},{18,10},{20,12},{22,14},{9,1... | collective-permute-start | bytes 5505032 | tf_op jit(solution)/shard_map/ppermute | solution.py:331
  19.5 49.2 %collective-permute-start.4 = (bf16[384,2048]{1,0:T(8,128)(2,1)}, bf16[384,2048]{1,0:T(8,128)(2,1)}, u32[]{:S(2)}, u32[]{:S(2)}) collective-permute-start(bf16[384,2048]{1,0:T(8,128)(2,1)} %constant_dynamic-slice_fusion.15), channel_id=1, source_target_pairs={{0,8},{2,10},{4,12},{6,14},{24,16},{26,18},{28,20},{30,22},{1,9},{... | collective-permute-start | bytes 4718600 | tf_op jit(solution)/shard_map/ppermute | solution.py:331
  27.2 23.3 %collective-permute-start = (bf16[256,1792]{1,0:T(8,128)(2,1)S(1)}, bf16[256,1792]{1,0:T(8,128)(2,1)S(1)}, u32[]{:S(2)}, u32[]{:S(2)}) collective-permute-start(bf16[256,1792]{1,0:T(8,128)(2,1)S(1)} %pad_maximum_fusion.8), channel_id=1, source_target_pairs={{0,4},{2,6},{4,0},{6,2},{8,12},{10,14},{12,8},{14,10},{16,20},{18,... | collective-permute-start | bytes 2752520 | tf_op jit(solution)/shard_map/ppermute | solution.py:334
  28.9 38.9 %collective-permute-start.1 = (bf16[256,1792]{1,0:T(8,128)(2,1)S(1)}, bf16[256,1792]{1,0:T(8,128)(2,1)S(1)}, u32[]{:S(2)}, u32[]{:S(2)}) collective-permute-start(bf16[256,1792]{1,0:T(8,128)(2,1)S(1)} %pad_maximum_fusion.9), channel_id=1, source_target_pairs={{0,6},{2,4},{4,2},{6,0},{8,14},{10,12},{12,10},{14,8},{16,22},{18,... | collective-permute-start | bytes 2752520 | tf_op jit(solution)/shard_map/ppermute | solution.py:334
  68.7 103.1 %all-gather.9.cloned.1.call-start = ((), (), s32[]{:S(2)}) async-start(), calls=%async_computation.1 | async-start | bytes 7864320 | tf_op jit(solution)/shard_map/all_gather | solution.py:341
  71.9 40.9 %collective-permute-start.6 = (bf16[512,1792]{1,0:T(8,128)(2,1)}, bf16[512,1792]{1,0:T(8,128)(2,1)}, u32[]{:S(2)}, u32[]{:S(2)}) collective-permute-start(bf16[512,1792]{1,0:T(8,128)(2,1)} %pad_maximum_fusion.1), channel_id=1, source_target_pairs={{8,16},{10,18},{12,20},{14,22},{16,8},{18,10},{20,12},{22,14},{9,1... | collective-permute-start | bytes 5505032 | tf_op jit(solution)/shard_map/ppermute | solution.py:331
  75.4 37.4 %collective-permute-start.7 = (bf16[1024,768]{1,0:T(8,128)(2,1)}, bf16[1024,768]{1,0:T(8,128)(2,1)}, u32[]{:S(2)}, u32[]{:S(2)}) collective-permute-start(bf16[1024,768]{1,0:T(8,128)(2,1)} %pad_maximum_fusion.4.refs_0_), channel_id=1, source_target_pairs={{0,8},{2,10},{4,12},{6,14},{8,0},{10,2},{12,4},{14,6},{16,24},{18,... | collective-permute-start | bytes 4718600 | tf_op jit(solution)/shard_map/ppermute | solution.py:331
  75.4 37.4 %collective-permute-start.8 = (bf16[384,2048]{1,0:T(8,128)(2,1)}, bf16[384,2048]{1,0:T(8,128)(2,1)}, u32[]{:S(2)}, u32[]{:S(2)}) collective-permute-start(bf16[384,2048]{1,0:T(8,128)(2,1)} %constant_dynamic-slice_fusion.15), channel_id=1, source_target_pairs={{0,4},{2,6},{4,0},{6,2},{8,12},{10,14},{12,8},{14,10},{16,20},{18,... | collective-permute-start | bytes 4718600 | tf_op jit(solution)/shard_map/ppermute | solution.py:334
  112.8 104.6 %all-gather.11.cloned.1.call-start = ((), (), s32[]{:S(2)}) async-start(), calls=%async_computation.2 | async-start | bytes 7864320 | tf_op jit(solution)/shard_map/all_gather | solution.py:341
  112.9 58.9 %collective-permute-start.13 = (bf16[1024,1024]{1,0:T(8,128)(2,1)S(1)}, bf16[1024,1024]{1,0:T(8,128)(2,1)}, u32[]{:S(2)}, u32[]{:S(2)}) collective-permute-start(bf16[1024,1024]{1,0:T(8,128)(2,1)S(1)} %pad_maximum_fusion.2.refs_0_), channel_id=1, source_target_pairs={{0,8},{2,10},{4,12},{6,14},{24,16},{26,18},{28,20},{30,22},{1,9},{... | collective-permute-start | bytes 6291464 | tf_op jit(solution)/shard_map/ppermute | solution.py:331
  118.6 53.1 %collective-permute-start.10 = (bf16[384,2048]{1,0:T(8,128)(2,1)}, bf16[384,2048]{1,0:T(8,128)(2,1)}, u32[]{:S(2)}, u32[]{:S(2)}) collective-permute-start(bf16[384,2048]{1,0:T(8,128)(2,1)} %collective-permute-done.4), channel_id=1, source_target_pairs={{0,4},{2,6},{4,0},{6,2},{8,12},{10,14},{12,8},{14,10},{16,20},{18,... | collective-permute-start | bytes 4718600 | tf_op jit(solution)/shard_map/ppermute | solution.py:334
  120.0 51.7 %collective-permute-start.12 = (bf16[1024,768]{1,0:T(8,128)(2,1)}, bf16[1024,768]{1,0:T(8,128)(2,1)}, u32[]{:S(2)}, u32[]{:S(2)}) collective-permute-start(bf16[1024,768]{1,0:T(8,128)(2,1)} %collective-permute-done.7.refs_1_), channel_id=1, source_target_pairs={{8,16},{10,18},{12,20},{14,22},{16,8},{18,10},{20,12},{22,14},{9,1... | collective-permute-start | bytes 4718600 | tf_op jit(solution)/shard_map/ppermute | solution.py:331
  124.8 47.0 %collective-permute-start.14 = (bf16[1024,768]{1,0:T(8,128)(2,1)}, bf16[1024,768]{1,0:T(8,128)(2,1)}, u32[]{:S(2)}, u32[]{:S(2)}) collective-permute-start(bf16[1024,768]{1,0:T(8,128)(2,1)} %pad_maximum_fusion.5.refs_2_), channel_id=1, source_target_pairs={{8,0},{10,2},{12,4},{14,6},{16,24},{18,26},{20,28},{22,30},{9,1},{... | collective-permute-start | bytes 4718600 | tf_op jit(solution)/shard_map/ppermute | solution.py:331
  126.1 45.7 %collective-permute-start.11 = (bf16[2,384,512]{2,1,0:T(8,128)(2,1)S(1)}, bf16[2,384,512]{2,1,0:T(8,128)(2,1)}, u32[]{:S(2)}, u32[]{:S(2)}) collective-permute-start(bf16[2,384,512]{2,1,0:T(8,128)(2,1)S(1)} %copy-done.14), channel_id=1, source_target_pairs={{0,4},{2,6},{4,0},{6,2},{8,12},{10,14},{12,8},{14,10},{16,20},{18,... | collective-permute-start | bytes 2359304 | tf_op jit(solution)/shard_map/ppermute | solution.py:334
  173.1 67.6 %collective-permute-start.20 = (bf16[1024,1024]{1,0:T(8,128)(2,1)}, bf16[1024,1024]{1,0:T(8,128)(2,1)}, u32[]{:S(2)}, u32[]{:S(2)}) collective-permute-start(bf16[1024,1024]{1,0:T(8,128)(2,1)} %collective-permute-done.13.refs_1_), channel_id=1, source_target_pairs={{8,16},{10,18},{12,20},{14,22},{16,8},{18,10},{20,12},{22,14},{9,1... | collective-permute-start | bytes 6291464 | tf_op jit(solution)/shard_map/ppermute | solution.py:331
  176.2 39.1 %collective-permute-start.17 = (bf16[1024,768]{1,0:T(8,128)(2,1)}, bf16[1024,768]{1,0:T(8,128)(2,1)}, u32[]{:S(2)}, u32[]{:S(2)}) collective-permute-start(bf16[1024,768]{1,0:T(8,128)(2,1)} %collective-permute-done.12.refs_0_), channel_id=1, source_target_pairs={{8,0},{10,2},{12,4},{14,6},{16,24},{18,26},{20,28},{22,30},{9,1},{... | collective-permute-start | bytes 4718600 | tf_op jit(solution)/shard_map/ppermute | solution.py:331
  177.8 62.9 %collective-permute-start.19 = (bf16[1536,512]{1,0:T(8,128)(2,1)S(1)}, bf16[1536,512]{1,0:T(8,128)(2,1)}, u32[]{:S(2)}, u32[]{:S(2)}) collective-permute-start(bf16[1536,512]{1,0:T(8,128)(2,1)S(1)} %pad_maximum_fusion.6.refs_10_.refs_11_.refs_12_.refs_13_), channel_id=1, source_target_pairs={{0,8},{2,10},{4,12},{6,14},{24,16},{26,18},{28,20},{30,22},{1,9},{... | collective-permute-start | bytes 4718600 | tf_op jit(solution)/shard_map/ppermute | solution.py:331
  184.6 9.9 %collective-permute-start.15 = (bf16[384,384]{1,0:T(8,128)(2,1)S(1)}, bf16[384,384]{1,0:T(8,128)(2,1)S(1)}, u32[]{:S(2)}, u32[]{:S(2)}) collective-permute-start(bf16[384,384]{1,0:T(8,128)(2,1)S(1)} %copy-done.16), channel_id=1, source_target_pairs={{0,4},{2,6},{4,0},{6,2},{8,12},{10,14},{12,8},{14,10},{16,20},{18,... | collective-permute-start | bytes 884744 | tf_op jit(solution)/shard_map/ppermute | solution.py:334
  186.2 12.7 %collective-permute-start.16 = (bf16[384,384]{1,0:T(8,128)(2,1)S(1)}, bf16[384,384]{1,0:T(8,128)(2,1)S(1)}, u32[]{:S(2)}, u32[]{:S(2)}) collective-permute-start(bf16[384,384]{1,0:T(8,128)(2,1)S(1)} %copy-done.15), channel_id=1, source_target_pairs={{0,6},{2,4},{4,2},{6,0},{8,14},{10,12},{12,10},{14,8},{16,22},{18,... | collective-permute-start | bytes 884744 | tf_op jit(solution)/shard_map/ppermute | solution.py:334
  244.6 6.4 %collective-permute-start.24 = (bf16[2,64,384]{2,1,0:T(8,128)(2,1)S(1)}, bf16[2,64,384]{2,1,0:T(8,128)(2,1)S(1)}, u32[]{:S(2)}, u32[]{:S(2)}) collective-permute-start(bf16[2,64,384]{2,1,0:T(8,128)(2,1)S(1)} %get-tuple-element.220), channel_id=1, source_target_pairs={{0,5},{1,4},{2,7},{3,6},{4,1},{5,0},{6,3},{7,2},{8,13},{9,12},{10,... | collective-permute-start | bytes 294920 | tf_op jit(solution)/shard_map/ppermute | solution.py:552
  246.2 6.4 %collective-permute-start.23 = (bf16[2,64,384]{2,1,0:T(8,128)(2,1)S(1)}, bf16[2,64,384]{2,1,0:T(8,128)(2,1)S(1)}, u32[]{:S(2)}, u32[]{:S(2)}) collective-permute-start(bf16[2,64,384]{2,1,0:T(8,128)(2,1)S(1)} %slice.214), channel_id=1, source_target_pairs={{0,4},{2,6},{4,0},{6,2},{8,12},{10,14},{12,8},{14,10},{16,20},{18,... | collective-permute-start | bytes 294920 | tf_op jit(solution)/shard_map/ppermute | solution.py:334
  252.7 6.7 %collective-permute-start.25 = (bf16[64,384]{1,0:T(8,128)(2,1)S(1)}, bf16[64,384]{1,0:T(8,128)(2,1)S(1)}, u32[]{:S(2)}, u32[]{:S(2)}) collective-permute-start(bf16[64,384]{1,0:T(8,128)(2,1)S(1)} %fusion.4), channel_id=1, source_target_pairs={{8,0},{10,2},{12,4},{14,6},{16,24},{18,26},{20,28},{22,30},{9,1},{... | collective-permute-start | bytes 147464 | tf_op jit(solution)/shard_map/ppermute | solution.py:331
  (23 other events, 173.4 us)
Sparse Core Ops, SparseCore 0:
  68.8 45.7 all-gather.6
  116.2 46.3 all-gather.8
  171.9 45.4 all-gather.10

commit v4 on v3

--- a/solution.py
+++ b/solution.py
@@ -129,7 +129,7 @@
         s, d = group["units"][0]
         d = d + r
         arrived(grad_buffer, grad_sem, n)
-        sig = 1.0 / (1.0 + jnp.exp(-gate))
+        sig = 0.5 * jnp.tanh(0.5 * gate) + 0.5
         cotangent = grad_buffer[n].astype(jnp.float32)
         grad_gate = (cotangent * up * sig * (1.0 + gate * (1.0 - sig))).astype(jnp.bfloat16)
         grad_up = (cotangent * gate * sig).astype(jnp.bfloat16)
@@ -491,18 +491,15 @@
         "b_next",
     )
     blocks_a = [(whole_a, 0), (end_a, 1), (far_a, 2)]
-    (held_late,) = ffn(
-        clock, 1, blocks_a, rows_in[:3], [group(own[2:], (0, 1, 2))], [], None, None, [], "a_second"
-    )
-    held_b, held_late, *side_grads_a = wait(held_b, held_late, *side_grads_a)
+    held_b, *side_grads_a = wait(held_b, *side_grads_a)
     grads_a = [(grads[0], 0, 0), (core_grads, 0, 0)] + [(piece, 0, 0) for piece in side_grads_a]
     sums = ffn(
         clock,
         1,
-        [(far_end_a, 3)],
+        [*blocks_a, (far_end_a, 3)],
         rows_in[:3],
-        [group(own, (0,), True)],
-        [held_a, held_late],
+        [group(own[:2], (3,), True), group(own[2:], (0, 1, 2, 3))],
+        [held_a],
         grads_a,
         proj_a,
         [],
@@ -539,7 +536,7 @@
 
     kept = jnp.stack([part[d] for part in sums for d in (0, 2)])
     sent = jnp.stack([part[d] for part in sums for d in (1, 3)])
-    kept = kept + flip(sent, 1)
+    kept = kept + flip(sent.astype(jnp.bfloat16), 1).astype(jnp.float32)
     keep = lax.dynamic_slice_in_dim(kept, x * ranks, ranks, 1)
     give = lax.dynamic_slice_in_dim(kept, (1 - x) * ranks, ranks, 1)
     send = give.astype(jnp.bfloat16)

time: 269 us -> 268 us (level)
    pallas_call x7 -> x6, Pallas kernels: 27.9 us -> 27.2 us  [ffn(): pl.pallas_call(functools.partial(ffn_kernel, cfg), out_shape=results, in_...]
  transfers between devices with their start and end apart: 29 -> 29, of which waited for: 13 -> 13; matrix products, arithmetic and copies ran while one was open for 11% -> 12% of each run, Pallas kernels for 10% -> 10%
where the time goes in v4:
time: 268 us; the launch traced here: 267 us
  waiting for transfers between devices  143 us (53%)
  starting transfers between devices  43.5 us (16%)
  Pallas kernels  29 us (11%)
  local copies, waits for them, and re-layouts  18 us (7%)
  other arithmetic  16 us (6%)
  between operations  14.3 us (5%)
  matrix products  3.61 us (1%)
    ppermute x13, waiting for transfers between devices, flip(): return lax.ppermute(value, 'dp', [(i, i ^ d) for i in range(16)])  90.5 us
    ppermute x11, waiting for transfers between devices, move(): return lax.ppermute(value, 'dp', perm)  47.4 us
    ppermute x11, starting transfers between devices, move(): return lax.ppermute(value, 'dp', perm)  31.8 us
    pallas_call x6, Pallas kernels, ffn(): pl.pallas_call(functools.partial(ffn_kernel, cfg), out_shape=results, in_...  27.2 us
    ppermute x13, starting transfers between devices, flip(): return lax.ppermute(value, 'dp', [(i, i ^ d) for i in range(16)])  8.34 us
  transfers between devices with their start and end apart: 29, of which 13 were waited for; matrix products, arithmetic and copies ran while one was open for 12% of the time, Pallas kernels for 10%

profile of v4, /device:TPU:0, one launch (start us, length us, event | category | flops | bytes accessed | tf_op | source)
XLA Modules:
  0.0 267.4 jit_solution(10141581428191765221)
XLA Ops:
  12.0 2.7 %constant_dynamic-slice_fusion.15 = bf16[384,2048]{1,0:T(8,128)(2,1)} fusion(bf16[384,4096]{1,0:T(8,128)(2,1)} %refs_4_.5, s32[]{:T(128)S(6)} %select_n.128), kind=kLoop, calls=%fused_computation.70 | loop fusion | bytes 3145732 | tf_op jit(solution)/shard_map/dynamic_slice | solution.py:391
  17.6 1.9 collective-permute-start.3
  19.5 7.6 %collective-permute-start.4 = (bf16[384,2048]{1,0:T(8,128)(2,1)}, bf16[384,2048]{1,0:T(8,128)(2,1)}, u32[]{:S(2)}, u32[]{:S(2)}) collective-permute-start(bf16[384,2048]{1,0:T(8,128)(2,1)} %constant_dynamic-slice_fusion.15), channel_id=1, source_target_pairs={{0,8},{2,10},{4,12},{6,14},{24,16},{26,18},{28,20},{30,22},{1,9},{... | collective-permute-start | bytes 4718600 | tf_op jit(solution)/shard_map/ppermute | solution.py:331
  28.9 3.6 %fusion.11.projected = f32[64,384]{1,0:T(8,128)} fusion(bf16[64,4096]{1,0:T(8,128)(2,1)S(1)} %copy-done, bf16[384,4096]{1,0:T(8,128)(2,1)} %refs_4_.5), kind=kOutput, calls=%fused_computation.85 | convolution fusion | flops 201326592 | bytes 3768320 | tf_op jit(solution)/shard_map/dot_general | solution.py:17
  32.5 18.0 %collective-permute-done = bf16[256,1792]{1,0:T(8,128)(2,1)S(1)} collective-permute-done((bf16[256,1792]{1,0:T(8,128)(2,1)S(1)}, bf16[256,1792]{1,0:T(8,128)(2,1)S(1)}, u32[]{:S(2)}, u32[]{:S(2)}) %collective-permute-start) | collective-permute-done | bytes 917536 | tf_op jit(solution)/shard_map/ppermute | solution.py:334
  50.5 17.2 %collective-permute-done.1 = bf16[256,1792]{1,0:T(8,128)(2,1)S(1)} collective-permute-done((bf16[256,1792]{1,0:T(8,128)(2,1)S(1)}, bf16[256,1792]{1,0:T(8,128)(2,1)S(1)}, u32[]{:S(2)}, u32[]{:S(2)}) %collective-permute-start.1) | collective-permute-done | bytes 917536 | tf_op jit(solution)/shard_map/ppermute | solution.py:334
  71.9 1.9 collective-permute-start.6
  79.8 1.9 constant_dynamic-slice_fusion.1
  84.8 28.0 %collective-permute-done.7.refs_1_ = bf16[1024,768]{1,0:T(8,128)(2,1)} collective-permute-done((bf16[1024,768]{1,0:T(8,128)(2,1)}, bf16[1024,768]{1,0:T(8,128)(2,1)}, u32[]{:S(2)}, u32[]{:S(2)}) %collective-permute-start.7) | collective-permute-done | bytes 1572896 | tf_op jit(solution)/shard_map/ppermute | solution.py:331
  112.9 5.7 %collective-permute-start.13 = (bf16[1024,1024]{1,0:T(8,128)(2,1)S(1)}, bf16[1024,1024]{1,0:T(8,128)(2,1)}, u32[]{:S(2)}, u32[]{:S(2)}) collective-permute-start(bf16[1024,1024]{1,0:T(8,128)(2,1)S(1)} %pad_maximum_fusion.2.refs_0_), channel_id=1, source_target_pairs={{0,8},{2,10},{4,12},{6,14},{24,16},{26,18},{28,20},{30,22},{1,9},{... | collective-permute-start | bytes 6291464 | tf_op jit(solution)/shard_map/ppermute | solution.py:331
  120.0 1.8 collective-permute-start.12
  127.2 1.7 broadcast_select_fusion.1
  131.1 40.6 %collective-permute-done.11 = bf16[2,384,512]{2,1,0:T(8,128)(2,1)} collective-permute-done((bf16[2,384,512]{2,1,0:T(8,128)(2,1)S(1)}, bf16[2,384,512]{2,1,0:T(8,128)(2,1)}, u32[]{:S(2)}, u32[]{:S(2)}) %collective-permute-start.11) | collective-permute-done | bytes 786464 | tf_op jit(solution)/shard_map/ppermute | solution.py:334
  173.1 2.0 collective-permute-start.20
  177.7 6.8 %collective-permute-start.19 = (bf16[1536,512]{1,0:T(8,128)(2,1)S(1)}, bf16[1536,512]{1,0:T(8,128)(2,1)}, u32[]{:S(2)}, u32[]{:S(2)}) collective-permute-start(bf16[1536,512]{1,0:T(8,128)(2,1)S(1)} %pad_maximum_fusion.6.refs_10_.refs_11_.refs_12_.refs_13_), channel_id=1, source_target_pairs={{0,8},{2,10},{4,12},{6,14},{24,16},{26,18},{28,20},{30,22},{1,9},{... | collective-permute-start | bytes 4718600 | tf_op jit(solution)/shard_map/ppermute | solution.py:331
  187.1 7.3 %collective-permute-done.15.refs_10_ = bf16[384,384]{1,0:T(8,128)(2,1)S(1)} collective-permute-done((bf16[384,384]{1,0:T(8,128)(2,1)S(1)}, bf16[384,384]{1,0:T(8,128)(2,1)S(1)}, u32[]{:S(2)}, u32[]{:S(2)}) %collective-permute-start.15) | collective-permute-done | bytes 294944 | tf_op jit(solution)/shard_map/ppermute | solution.py:334
  194.4 4.4 %collective-permute-done.16.refs_11_ = bf16[384,384]{1,0:T(8,128)(2,1)S(1)} collective-permute-done((bf16[384,384]{1,0:T(8,128)(2,1)S(1)}, bf16[384,384]{1,0:T(8,128)(2,1)S(1)}, u32[]{:S(2)}, u32[]{:S(2)}) %collective-permute-start.16) | collective-permute-done | bytes 294944 | tf_op jit(solution)/shard_map/ppermute | solution.py:334
  200.3 14.9 %collective-permute-done.17 = bf16[1024,768]{1,0:T(8,128)(2,1)} collective-permute-done((bf16[1024,768]{1,0:T(8,128)(2,1)}, bf16[1024,768]{1,0:T(8,128)(2,1)}, u32[]{:S(2)}, u32[]{:S(2)}) %collective-permute-start.17) | collective-permute-done | bytes 1572896 | tf_op jit(solution)/shard_map/ppermute | solution.py:331
  215.3 2.1 all-gather.11.cloned.1.call-done
  217.4 23.1 %conditional.1 = (f32[4,128,384]{2,1,0:T(8,128)S(1)}) conditional(s32[]{:T(128)} %convert_element_type.28, (s32[6]{0:T(128)S(1)}, bf16[1024,768]{1,0:T(8,128)(2,1)}, bf16[1024,768]{1,0:T(8,128)(2,1)}, bf16[1024,768]{1,0:T(8,128)(2,1)}, bf16[1024,768]{1,0:T(8,128)(2,1)}, /*index=5*/bf16[384,4096]{1,0:T(8,128)(2,1)}, bf16[384,4096]{1,0:T(8,128)(2,1)}, ...), branch_computations={%region_0.1_spmd, %region_1.2_spmd} | conditional | flops 1 | bytes 1572873 | solution.py:520
  217.5 23.1 %a_end.1 = f32[4,128,384]{2,1,0:T(8,128)S(1)} custom-call(s32[6]{0:T(128)S(1)} %get-tuple-element.34.idx, bf16[1024,768]{1,0:T(8,128)(2,1)} %get-tuple-element.35.refs_0_, bf16[1024,768]{1,0:T(8,128)(2,1)} %get-tuple-element.36.refs_1_, bf16[1024,768]{1,0:T(8,128)(2,1)} %get-tuple-element.37.refs_2_, bf16[1024,768]{1,0:T(8,128)(2,1)} %get-tuple-element.38.refs_3_, ...), custom_call_target="tpu_custom_call" | custom-call | flops 1 | bytes 1 | tf_op jit(solution)/shard_map/cond/branch_0_fun/a_end/pallas_call | solution.py:279
  247.6 2.7 %collective-permute-done.24 = bf16[2,64,384]{2,1,0:T(8,128)(2,1)S(1)} collective-permute-done((bf16[2,64,384]{2,1,0:T(8,128)(2,1)S(1)}, bf16[2,64,384]{2,1,0:T(8,128)(2,1)S(1)}, u32[]{:S(2)}, u32[]{:S(2)}) %collective-permute-start.24) | collective-permute-done | bytes 98336 | tf_op jit(solution)/shard_map/ppermute | solution.py:549
  254.0 4.5 %collective-permute-done.25.sent = bf16[64,384]{1,0:T(8,128)(2,1)S(1)} collective-permute-done((bf16[64,384]{1,0:T(8,128)(2,1)S(1)}, bf16[64,384]{1,0:T(8,128)(2,1)S(1)}, u32[]{:S(2)}, u32[]{:S(2)}) %collective-permute-start.25) | collective-permute-done | bytes 49184 | tf_op jit(solution)/shard_map/ppermute | solution.py:331
  259.1 1.8 features.1
  (133 shorter events, 50.7 us)
Async XLA Ops:
  7.2 123.3 %all-gather.7.cloned.1.call-start = ((), (), s32[]{:S(2)}) async-start(), calls=%async_computation | async-start | bytes 7864320 | tf_op jit(solution)/shard_map/all_gather | solution.py:341
  10.2 58.5 %collective-permute-start.5 = (bf16[384,4096]{1,0:T(8,128)(2,1)}, bf16[384,4096]{1,0:T(8,128)(2,1)}, u32[]{:S(2)}, u32[]{:S(2)}) collective-permute-start(bf16[384,4096]{1,0:T(8,128)(2,1)} %refs_4_.5), channel_id=1, source_target_pairs={{0,2},{2,0},{4,6},{6,4},{8,10},{10,8},{12,14},{14,12},{16,18},{18,... | collective-permute-start | bytes 9437192 | tf_op jit(solution)/shard_map/ppermute | solution.py:334
  17.6 51.1 %collective-permute-start.3 = (bf16[512,1792]{1,0:T(8,128)(2,1)}, bf16[512,1792]{1,0:T(8,128)(2,1)}, u32[]{:S(2)}, u32[]{:S(2)}) collective-permute-start(bf16[512,1792]{1,0:T(8,128)(2,1)} %pad_maximum_fusion), channel_id=1, source_target_pairs={{8,16},{10,18},{12,20},{14,22},{16,8},{18,10},{20,12},{22,14},{9,1... | collective-permute-start | bytes 5505032 | tf_op jit(solution)/shard_map/ppermute | solution.py:331
  19.5 49.2 %collective-permute-start.4 = (bf16[384,2048]{1,0:T(8,128)(2,1)}, bf16[384,2048]{1,0:T(8,128)(2,1)}, u32[]{:S(2)}, u32[]{:S(2)}) collective-permute-start(bf16[384,2048]{1,0:T(8,128)(2,1)} %constant_dynamic-slice_fusion.15), channel_id=1, source_target_pairs={{0,8},{2,10},{4,12},{6,14},{24,16},{26,18},{28,20},{30,22},{1,9},{... | collective-permute-start | bytes 4718600 | tf_op jit(solution)/shard_map/ppermute | solution.py:331
  27.2 23.3 %collective-permute-start = (bf16[256,1792]{1,0:T(8,128)(2,1)S(1)}, bf16[256,1792]{1,0:T(8,128)(2,1)S(1)}, u32[]{:S(2)}, u32[]{:S(2)}) collective-permute-start(bf16[256,1792]{1,0:T(8,128)(2,1)S(1)} %pad_maximum_fusion.8), channel_id=1, source_target_pairs={{0,4},{2,6},{4,0},{6,2},{8,12},{10,14},{12,8},{14,10},{16,20},{18,... | collective-permute-start | bytes 2752520 | tf_op jit(solution)/shard_map/ppermute | solution.py:334
  28.8 38.9 %collective-permute-start.1 = (bf16[256,1792]{1,0:T(8,128)(2,1)S(1)}, bf16[256,1792]{1,0:T(8,128)(2,1)S(1)}, u32[]{:S(2)}, u32[]{:S(2)}) collective-permute-start(bf16[256,1792]{1,0:T(8,128)(2,1)S(1)} %pad_maximum_fusion.9), channel_id=1, source_target_pairs={{0,6},{2,4},{4,2},{6,0},{8,14},{10,12},{12,10},{14,8},{16,22},{18,... | collective-permute-start | bytes 2752520 | tf_op jit(solution)/shard_map/ppermute | solution.py:334
  68.7 103.1 %all-gather.9.cloned.1.call-start = ((), (), s32[]{:S(2)}) async-start(), calls=%async_computation.1 | async-start | bytes 7864320 | tf_op jit(solution)/shard_map/all_gather | solution.py:341
  71.9 40.9 %collective-permute-start.6 = (bf16[512,1792]{1,0:T(8,128)(2,1)}, bf16[512,1792]{1,0:T(8,128)(2,1)}, u32[]{:S(2)}, u32[]{:S(2)}) collective-permute-start(bf16[512,1792]{1,0:T(8,128)(2,1)} %pad_maximum_fusion.1), channel_id=1, source_target_pairs={{8,16},{10,18},{12,20},{14,22},{16,8},{18,10},{20,12},{22,14},{9,1... | collective-permute-start | bytes 5505032 | tf_op jit(solution)/shard_map/ppermute | solution.py:331
  75.4 37.4 %collective-permute-start.7 = (bf16[1024,768]{1,0:T(8,128)(2,1)}, bf16[1024,768]{1,0:T(8,128)(2,1)}, u32[]{:S(2)}, u32[]{:S(2)}) collective-permute-start(bf16[1024,768]{1,0:T(8,128)(2,1)} %pad_maximum_fusion.4.refs_0_), channel_id=1, source_target_pairs={{0,8},{2,10},{4,12},{6,14},{8,0},{10,2},{12,4},{14,6},{16,24},{18,... | collective-permute-start | bytes 4718600 | tf_op jit(solution)/shard_map/ppermute | solution.py:331
  75.4 37.4 %collective-permute-start.8 = (bf16[384,2048]{1,0:T(8,128)(2,1)}, bf16[384,2048]{1,0:T(8,128)(2,1)}, u32[]{:S(2)}, u32[]{:S(2)}) collective-permute-start(bf16[384,2048]{1,0:T(8,128)(2,1)} %constant_dynamic-slice_fusion.15), channel_id=1, source_target_pairs={{0,4},{2,6},{4,0},{6,2},{8,12},{10,14},{12,8},{14,10},{16,20},{18,... | collective-permute-start | bytes 4718600 | tf_op jit(solution)/shard_map/ppermute | solution.py:334
  112.8 104.6 %all-gather.11.cloned.1.call-start = ((), (), s32[]{:S(2)}) async-start(), calls=%async_computation.2 | async-start | bytes 7864320 | tf_op jit(solution)/shard_map/all_gather | solution.py:341
  112.9 58.9 %collective-permute-start.13 = (bf16[1024,1024]{1,0:T(8,128)(2,1)S(1)}, bf16[1024,1024]{1,0:T(8,128)(2,1)}, u32[]{:S(2)}, u32[]{:S(2)}) collective-permute-start(bf16[1024,1024]{1,0:T(8,128)(2,1)S(1)} %pad_maximum_fusion.2.refs_0_), channel_id=1, source_target_pairs={{0,8},{2,10},{4,12},{6,14},{24,16},{26,18},{28,20},{30,22},{1,9},{... | collective-permute-start | bytes 6291464 | tf_op jit(solution)/shard_map/ppermute | solution.py:331
  118.6 53.1 %collective-permute-start.10 = (bf16[384,2048]{1,0:T(8,128)(2,1)}, bf16[384,2048]{1,0:T(8,128)(2,1)}, u32[]{:S(2)}, u32[]{:S(2)}) collective-permute-start(bf16[384,2048]{1,0:T(8,128)(2,1)} %collective-permute-done.4), channel_id=1, source_target_pairs={{0,4},{2,6},{4,0},{6,2},{8,12},{10,14},{12,8},{14,10},{16,20},{18,... | collective-permute-start | bytes 4718600 | tf_op jit(solution)/shard_map/ppermute | solution.py:334
  120.0 51.7 %collective-permute-start.12 = (bf16[1024,768]{1,0:T(8,128)(2,1)}, bf16[1024,768]{1,0:T(8,128)(2,1)}, u32[]{:S(2)}, u32[]{:S(2)}) collective-permute-start(bf16[1024,768]{1,0:T(8,128)(2,1)} %collective-permute-done.7.refs_1_), channel_id=1, source_target_pairs={{8,16},{10,18},{12,20},{14,22},{16,8},{18,10},{20,12},{22,14},{9,1... | collective-permute-start | bytes 4718600 | tf_op jit(solution)/shard_map/ppermute | solution.py:331
  124.7 47.0 %collective-permute-start.14 = (bf16[1024,768]{1,0:T(8,128)(2,1)}, bf16[1024,768]{1,0:T(8,128)(2,1)}, u32[]{:S(2)}, u32[]{:S(2)}) collective-permute-start(bf16[1024,768]{1,0:T(8,128)(2,1)} %pad_maximum_fusion.5.refs_2_), channel_id=1, source_target_pairs={{8,0},{10,2},{12,4},{14,6},{16,24},{18,26},{20,28},{22,30},{9,1},{... | collective-permute-start | bytes 4718600 | tf_op jit(solution)/shard_map/ppermute | solution.py:331
  126.0 45.7 %collective-permute-start.11 = (bf16[2,384,512]{2,1,0:T(8,128)(2,1)S(1)}, bf16[2,384,512]{2,1,0:T(8,128)(2,1)}, u32[]{:S(2)}, u32[]{:S(2)}) collective-permute-start(bf16[2,384,512]{2,1,0:T(8,128)(2,1)S(1)} %copy-done.14), channel_id=1, source_target_pairs={{0,4},{2,6},{4,0},{6,2},{8,12},{10,14},{12,8},{14,10},{16,20},{18,... | collective-permute-start | bytes 2359304 | tf_op jit(solution)/shard_map/ppermute | solution.py:334
  173.1 67.5 %collective-permute-start.20 = (bf16[1024,1024]{1,0:T(8,128)(2,1)}, bf16[1024,1024]{1,0:T(8,128)(2,1)}, u32[]{:S(2)}, u32[]{:S(2)}) collective-permute-start(bf16[1024,1024]{1,0:T(8,128)(2,1)} %collective-permute-done.13.refs_1_), channel_id=1, source_target_pairs={{8,16},{10,18},{12,20},{14,22},{16,8},{18,10},{20,12},{22,14},{9,1... | collective-permute-start | bytes 6291464 | tf_op jit(solution)/shard_map/ppermute | solution.py:331
  176.1 39.1 %collective-permute-start.17 = (bf16[1024,768]{1,0:T(8,128)(2,1)}, bf16[1024,768]{1,0:T(8,128)(2,1)}, u32[]{:S(2)}, u32[]{:S(2)}) collective-permute-start(bf16[1024,768]{1,0:T(8,128)(2,1)} %collective-permute-done.12.refs_3_), channel_id=1, source_target_pairs={{8,0},{10,2},{12,4},{14,6},{16,24},{18,26},{20,28},{22,30},{9,1},{... | collective-permute-start | bytes 4718600 | tf_op jit(solution)/shard_map/ppermute | solution.py:331
  177.7 62.9 %collective-permute-start.19 = (bf16[1536,512]{1,0:T(8,128)(2,1)S(1)}, bf16[1536,512]{1,0:T(8,128)(2,1)}, u32[]{:S(2)}, u32[]{:S(2)}) collective-permute-start(bf16[1536,512]{1,0:T(8,128)(2,1)S(1)} %pad_maximum_fusion.6.refs_10_.refs_11_.refs_12_.refs_13_), channel_id=1, source_target_pairs={{0,8},{2,10},{4,12},{6,14},{24,16},{26,18},{28,20},{30,22},{1,9},{... | collective-permute-start | bytes 4718600 | tf_op jit(solution)/shard_map/ppermute | solution.py:331
  184.5 9.9 %collective-permute-start.15 = (bf16[384,384]{1,0:T(8,128)(2,1)S(1)}, bf16[384,384]{1,0:T(8,128)(2,1)S(1)}, u32[]{:S(2)}, u32[]{:S(2)}) collective-permute-start(bf16[384,384]{1,0:T(8,128)(2,1)S(1)} %copy-done.16), channel_id=1, source_target_pairs={{0,4},{2,6},{4,0},{6,2},{8,12},{10,14},{12,8},{14,10},{16,20},{18,... | collective-permute-start | bytes 884744 | tf_op jit(solution)/shard_map/ppermute | solution.py:334
  186.2 12.7 %collective-permute-start.16 = (bf16[384,384]{1,0:T(8,128)(2,1)S(1)}, bf16[384,384]{1,0:T(8,128)(2,1)S(1)}, u32[]{:S(2)}, u32[]{:S(2)}) collective-permute-start(bf16[384,384]{1,0:T(8,128)(2,1)S(1)} %copy-done.15), channel_id=1, source_target_pairs={{0,6},{2,4},{4,2},{6,0},{8,14},{10,12},{12,10},{14,8},{16,22},{18,... | collective-permute-start | bytes 884744 | tf_op jit(solution)/shard_map/ppermute | solution.py:334
  243.9 6.4 %collective-permute-start.24 = (bf16[2,64,384]{2,1,0:T(8,128)(2,1)S(1)}, bf16[2,64,384]{2,1,0:T(8,128)(2,1)S(1)}, u32[]{:S(2)}, u32[]{:S(2)}) collective-permute-start(bf16[2,64,384]{2,1,0:T(8,128)(2,1)S(1)} %get-tuple-element.218), channel_id=1, source_target_pairs={{0,5},{1,4},{2,7},{3,6},{4,1},{5,0},{6,3},{7,2},{8,13},{9,12},{10,... | collective-permute-start | bytes 294920 | tf_op jit(solution)/shard_map/ppermute | solution.py:549
  245.6 6.4 %collective-permute-start.23 = (bf16[2,64,384]{2,1,0:T(8,128)(2,1)S(1)}, bf16[2,64,384]{2,1,0:T(8,128)(2,1)S(1)}, u32[]{:S(2)}, u32[]{:S(2)}) collective-permute-start(bf16[2,64,384]{2,1,0:T(8,128)(2,1)S(1)} %slice.218), channel_id=1, source_target_pairs={{0,4},{2,6},{4,0},{6,2},{8,12},{10,14},{12,8},{14,10},{16,20},{18,... | collective-permute-start | bytes 294920 | tf_op jit(solution)/shard_map/ppermute | solution.py:334
  252.1 6.4 %collective-permute-start.25 = (bf16[64,384]{1,0:T(8,128)(2,1)S(1)}, bf16[64,384]{1,0:T(8,128)(2,1)S(1)}, u32[]{:S(2)}, u32[]{:S(2)}) collective-permute-start(bf16[64,384]{1,0:T(8,128)(2,1)S(1)} %fusion.4), channel_id=1, source_target_pairs={{8,0},{10,2},{12,4},{14,6},{16,24},{18,26},{20,28},{22,30},{9,1},{... | collective-permute-start | bytes 147464 | tf_op jit(solution)/shard_map/ppermute | solution.py:331
  (23 other events, 172.7 us)
Sparse Core Ops, SparseCore 0:
  68.8 45.7 all-gather.6
  116.2 46.3 all-gather.8
  171.9 45.4 all-gather.10
